TPU v7x, 128 devices: a whole 4x4x4 slice. The times are simulated.
128 devices in a mesh: section: 2 (over x_lo), cache: 16 (over y, x_hi, core), mp: 4 (over z).
Axes of the slice: x: 4 (x_hi: 2, x_lo: 2; x = x_hi * 2 + x_lo), y: 4, z: 4, core: 2. Of those that a mesh axis runs over, the one named last changes fastest.
Arguments:
- x_in: bfloat16 [16, 2048, 8192], P('cache', 'section', 'mp'), may hold values from -6 to 6
- z_in: bfloat16 [16, 2048, 8192], P('cache', 'section', 'mp'), may hold values from -6 to 6
- bc_in: bfloat16 [16, 2048, 8, 256], P('cache', 'section', 'mp'), may hold values from -6 to 6
- dt_in: bfloat16 [16, 2048, 128], P('cache', 'section', 'mp'), may hold values from -4 to 4
- tail_x: bfloat16 [16, 3, 8192], P('cache', None, 'mp'), may hold values from -6 to 6
- tail_bc: bfloat16 [16, 3, 8, 256], P('cache', None, 'mp'), may hold values from -6 to 6
- conv_w_x: float32 [4, 8192], P(None, 'mp'), may hold values from -3 to 3
- conv_b_x: float32 [8192], P('mp'), may hold values from -3 to 3
- conv_w_bc: float32 [4, 8, 256], P(None, 'mp'), may hold values from -3 to 3
- conv_b_bc: float32 [8, 256], P('mp'), may hold values from -3 to 3
- dt_bias: float32 [128], P('mp'), may hold values from -1 to 1
- decay_rate: float32 [128], P('mp'), may hold values from 0.00024414062 to 0.0234375
- norm_gain: float32 [8192], P('mp'), may hold values from 0.5 to 1.5
- state_pool: float32 [16384, 64, 128], P(('section', 'cache', 'mp')), may hold values from -48 to 48
- block_slots: int32 [16, 128], replicated, may hold values from 0 to 16383, as said below
- new_len: int32 [16], P('cache'), may hold values from 512 to 2048, as said below
Outputs:
- gated_out: bfloat16 [16, 2048, 8192], P('cache', 'section', 'mp')
- final_state: float32 [16, 4, 2, 16, 64, 128], P('cache', 'mp', 'section')
Inputs may be any that keep to these rules, and one draw needn't show every extreme that they name: `block_slots`: entry [r, h] is the slot of state_pool holding request r's cached state of head h; all entries differ. That slot lies on a device of section index (h mod (32)) // 16. Of the cached states that one section index needs for the requests of one cache index and the heads of one mp index, at most 2 lie on one device, and in each such set some device holds exactly 2. Positions from new_len[r] on are padding; some request fills all 2048 positions.
All inputs are finite; a program needn't handle non-finite values.
Results may differ from a plain program's by a relative error of at most 0.0085.
Values may be sent and summed in bfloat16 or wider, within the bound.
No kernel may reach another device: no remote copies, remote signals or barrier semaphores. Data moves between devices by JAX's collectives and lax.ppermute only.
A program may use at most 128 MiB of HBM per device.

v0:
```python
import jax
import jax.numpy as jnp
from jax import lax
from jax.sharding import PartitionSpec as P

BLK = 128


EPS = 1e-05


def from_behind(block, axis, distance):
    devices = range(lax.axis_size(axis))
    route = [(i - distance, i) for i in devices if i - distance in devices]
    return lax.ppermute(block, axis, route)


def carried_in(part, axis, combine, identity):
    place = lax.axis_index(axis)
    gathered = jax.tree.map(lambda a: lax.all_gather(a, axis), part)
    state = jax.tree.map(lambda a, e: jnp.zeros_like(a) + jnp.asarray(e, a.dtype), part, identity)

    def one(step, state):
        return combine(
            state, jax.tree.map(lambda a: lax.dynamic_index_in_dim(a, step, 0, False), gathered)
        )

    return lax.fori_loop(0, place, one, state)


def from_root(value, axis, root):
    mine = lax.axis_index(axis) == root
    return lax.psum(jnp.where(mine, value, jnp.zeros_like(value)), axis)


def conv_part(leading, values, kernel, offset):
    joined = jnp.concatenate([leading, values], 1).astype(jnp.float32)
    length = values.shape[1]
    summed = offset + sum((kernel[k] * joined[:, k : k + length] for k in range(kernel.shape[0])))
    return jax.nn.silu(summed).astype(jnp.bfloat16)


def combine_carry(earlier, later):
    return (earlier[0] * later[0], later[0][..., None, None] * earlier[1] + later[1])


def body(
    x_in,
    z_in,
    bc_in,
    dt_in,
    tail_x,
    tail_bc,
    conv_w_x,
    conv_b_x,
    conv_w_bc,
    conv_b_bc,
    dt_bias,
    decay_rate,
    norm_gain,
    state_pool,
    block_slots,
    new_len,
):
    section_idx = lax.axis_index("section")
    section_count = lax.axis_size("section")
    cache_count = lax.axis_size("cache")
    mp_count = lax.axis_size("mp")
    peer_count = cache_count * mp_count
    peer_self = lax.axis_index("cache") * mp_count + lax.axis_index("mp")
    requests, seg_len, channels = x_in.shape
    group_count = bc_in.shape[2]
    state_size = bc_in.shape[3] // 2
    head_count = dt_in.shape[2]
    per_group = head_count // group_count
    head_dim = channels // head_count
    rim_len = conv_w_x.shape[0] - 1
    quarter = head_count // section_count
    prior_x, prior_bc = from_behind(
        (x_in[:, seg_len - rim_len :], bc_in[:, seg_len - rim_len :]), "section", 1
    )
    at_start = section_idx == 0
    prior_x = jnp.where(at_start, tail_x, prior_x)
    prior_bc = jnp.where(at_start, tail_bc, prior_bc)
    x_conv = conv_part(prior_x, x_in, conv_w_x, conv_b_x)
    bc_conv = conv_part(prior_bc, bc_in, conv_w_bc, conv_b_bc)
    positions = section_idx * seg_len + jnp.arange(seg_len, dtype=jnp.int32)
    live_mask = (positions[None, :] < new_len[:, None]).astype(jnp.float32)
    step_size = jax.nn.softplus(dt_in.astype(jnp.float32) + dt_bias) * live_mask[..., None]
    log_decay = -step_size * decay_rate
    causal = jnp.arange(BLK)[:, None] >= jnp.arange(BLK)[None, :]
    blocks_done = []
    total_decay = jnp.ones((requests, group_count, per_group), jnp.float32)
    summary = jnp.zeros((requests, group_count, per_group, head_dim, state_size), jnp.float32)
    for block_num in range(seg_len // BLK):
        window = slice(block_num * BLK, (block_num + 1) * BLK)
        x_block = x_conv[:, window].reshape(requests, BLK, group_count, per_group, head_dim)
        b_block = bc_conv[:, window, :, :state_size]
        c_block = bc_conv[:, window, :, state_size:]
        a_block = log_decay[:, window].reshape(requests, BLK, group_count, per_group)
        dt_block = step_size[:, window].reshape(requests, BLK, group_count, per_group)
        cum_log = jnp.cumsum(a_block, 1)
        scores = jnp.einsum("rtgn,rsgn->rgts", c_block, b_block, preferred_element_type=jnp.float32)
        cum_heads = cum_log.transpose(0, 2, 3, 1)
        log_gap = cum_heads[..., :, None] - cum_heads[..., None, :]
        decays = jnp.where(causal, jnp.exp(jnp.where(causal, log_gap, 0.0)), 0.0)
        weights = (
            scores[:, :, None] * decays * dt_block.transpose(0, 2, 3, 1)[..., None, :]
        ).astype(jnp.bfloat16)
        y_intra = jnp.einsum(
            "rgkts,rsgkp->rtgkp", weights, x_block, preferred_element_type=jnp.float32
        )
        tail_weight = jnp.exp(cum_log[:, -1:] - cum_log) * dt_block
        x_weighted = (x_block.astype(jnp.float32) * tail_weight[..., None]).astype(jnp.bfloat16)
        contribution = jnp.einsum(
            "rsgkp,rsgn->rgkpn", x_weighted, b_block, preferred_element_type=jnp.float32
        )
        block_decay = jnp.exp(cum_log[:, -1])
        summary = block_decay[..., None, None] * summary + contribution
        total_decay = total_decay * block_decay
        blocks_done.append(
            (
                c_block,
                cum_log,
                y_intra,
                contribution,
                block_decay,
                z_in[:, window],
                live_mask[:, window],
            )
        )
    slots_dev = state_pool.shape[0]
    most_held = slots_dev // peer_count
    per_dest = requests * quarter
    listed = block_slots.reshape(cache_count, requests, mp_count, section_count, quarter)
    listed = lax.dynamic_index_in_dim(listed, section_idx, 3, keepdims=False)
    listed = listed.transpose(0, 2, 1, 3).reshape(peer_count, per_dest)
    owner_peer = listed // slots_dev % peer_count
    local_slot = listed % slots_dev
    one_hot = (owner_peer[..., None] == jnp.arange(peer_count, dtype=jnp.int32)).astype(jnp.int32)
    position = jnp.sum((jnp.cumsum(one_hot, 1) - one_hot) * one_hot, -1)
    chosen = (owner_peer[:, None, :] == peer_self) & (
        position[:, None, :] == jnp.arange(most_held, dtype=jnp.int32)[None, :, None]
    )
    picked = jnp.sum(jnp.where(chosen, local_slot[:, None, :], 0), -1)
    present = jnp.any(chosen, -1)
    outgoing = jnp.where(present[..., None, None], state_pool[picked], 0.0)
    incoming = lax.all_to_all(outgoing, ("cache", "mp"), split_axis=0, concat_axis=0, tiled=True)
    own_owner = lax.dynamic_index_in_dim(owner_peer, peer_self, 0, keepdims=False)
    own_position = lax.dynamic_index_in_dim(position, peer_self, 0, keepdims=False)
    fetched = incoming.reshape(peer_count * most_held, head_dim, state_size)[
        own_owner * most_held + own_position
    ]
    start_quarter = fetched.reshape(requests, quarter, head_dim, state_size)
    decay_heads = total_decay.reshape(requests, head_count)
    summary_heads = summary.reshape(requests, head_count, head_dim, state_size)
    start_all = lax.all_gather(start_quarter, "section", axis=1, tiled=True)
    identity = (jnp.ones_like(decay_heads), jnp.zeros_like(summary_heads))
    before_decay, before_state = carried_in(
        (decay_heads, summary_heads), "section", combine_carry, identity
    )
    device_start = before_decay[..., None, None] * start_all + before_state
    carried = device_start.reshape(requests, group_count, per_group, head_dim, state_size)
    outputs = []
    for c_block, cum_log, y_intra, contribution, block_decay, z_window, live_window in blocks_done:
        y_inter = jnp.exp(cum_log)[..., None] * jnp.einsum(
            "rtgn,rgkpn->rtgkp",
            c_block,
            carried.astype(jnp.bfloat16),
            preferred_element_type=jnp.float32,
        )
        y_all = y_intra + y_inter
        carried = block_decay[..., None, None] * carried + contribution
        gated_vals = y_all.reshape(requests, BLK, channels) * jax.nn.silu(
            z_window.astype(jnp.float32)
        )
        grouped = gated_vals.reshape(requests, BLK, group_count, channels // group_count)
        inverse_rms = lax.rsqrt(jnp.mean(grouped * grouped, -1, keepdims=True) + EPS)
        result = (
            (grouped * inverse_rms).reshape(requests, BLK, channels)
            * norm_gain
            * live_window[..., None]
        )
        outputs.append(result.astype(jnp.bfloat16))
    gated_out = jnp.concatenate(outputs, 1)
    whole_end = from_root(
        carried.reshape(requests, head_count, head_dim, state_size), "section", section_count - 1
    )
    final_quarter = lax.dynamic_slice_in_dim(whole_end, section_idx * quarter, quarter, 1)
    return (gated_out, final_quarter.reshape(requests, 1, 1, quarter, head_dim, state_size))


def solution(mesh):
    in_specs = (
        P("cache", "section", "mp"),
        P("cache", "section", "mp"),
        P("cache", "section", "mp", None),
        P("cache", "section", "mp"),
        P("cache", None, "mp"),
        P("cache", None, "mp", None),
        P(None, "mp"),
        P("mp"),
        P(None, "mp", None),
        P("mp", None),
        P("mp"),
        P("mp"),
        P("mp"),
        P(("section", "cache", "mp"), None, None),
        P(),
        P("cache"),
    )
    out_specs = (P("cache", "section", "mp"), P("cache", "mp", "section", None, None, None))
    return jax.shard_map(body, mesh=mesh, in_specs=in_specs, out_specs=out_specs, check_vma=False)
```

profile of v0, /device:TPU:1, one launch (start us, length us, event | category | flops | bytes accessed | tf_op | source)
XLA Modules:
  0.0 310.2 jit_solution(429901567510444490)
XLA Ops:
  8.6 4.5 %collective-permute-start = (bf16[1,3,2048]{2,1,0:T(4,128)(2,1)}, bf16[1,3,2048]{2,1,0:T(4,128)(2,1)}, u32[]{:S(2)}, u32[]{:S(2)}) collective-permute-start(bf16[1,3,2048]{2,1,0:T(4,128)(2,1)} %slice.271), channel_id=1, source_target_pairs={{0,64},{1,65},{2,66},{3,67},{4,68},{5,69},{6,70},{7,71},{8,72},{9,... | collective-permute-start | bytes 36872 | tf_op jit(solution)/shard_map/ppermute | solution.py:15
  17.3 5.0 %gather_fusion = f32[128,64,128]{2,1,0:T(8,128)} fusion(f32[128,64,128]{2,1,0:T(8,128)} %param.31, s32[1024]{0:T(1024)S(1)} %pad_clamp_fusion.1), kind=kCustom, calls=%fused_computation | custom fusion | bytes 8389120 | tf_op jit(solution)/shard_map/gather | solution.py:147
  22.3 4.6 %broadcast_select_fusion = f32[64,2,64,128]{3,2,1,0:T(8,128)} fusion(f32[64,2,64,128]{3,2,1,0:T(8,128)} %bitcast.494, pred[64,2]{1,0:T(8,128)(4,1)S(1)} %copy.478), kind=kLoop, calls=%fused_computation.31 | loop fusion | flops 1048576 | bytes 8388736 | tf_op jit(solution)/shard_map/jit(_where)/select_n | solution.py:147
  26.8 11.9 %all-to-all-start = ((f32[64,2,64,128]{3,2,1,0:T(8,128)}), f32[64,2,64,128]{3,2,1,0:T(8,128)}, u32[]{:S(2)}, u32[]{:S(2)}) async-start(f32[64,2,64,128]{3,2,1,0:T(8,128)} %broadcast_select_fusion), calls=%async_computation | async-start | bytes 8388608 | tf_op jit(solution)/shard_map/all_to_all | solution.py:148
  59.2 5.4 %multiply_convert_fusion = bf16[1,1024,2048]{2,1,0:T(8,128)(2,1)S(1)} fusion(f32[1,1027,2048]{2,1,0:T(8,128)S(1)} %maximum_convert_fusion, f32[2048]{0:T(1024)S(1)} %bitcast.559, f32[2048]{0:T(1024)S(1)} %bitcast.560, f32[2048]{0:T(1024)S(1)} %bitcast.558, f32[2048]{0:T(1024)S(1)} %bitcast.557, f32[2048]{0:T(1024)S(1)} %copy-done.102), kind=kLoop, calls=%fused_computation.14 | loop fusion | flops 27262976 | bytes 37789696 | tf_op jit(solution)/shard_map/convert_element_type | solution.py:40
  97.2 3.5 %all_gather.9 = f32[2,1,32]{2,1,0:T(1,128)} all-gather(f32[1,1,32]{2,1,0:T(1,128)S(1)} %reshape.1761), channel_id=1, replica_groups=mesh['section'=2,'cache'=16,'mp'=4] {'section'}, dimensions={0}, use_global_device_ids=true | all-gather | bytes 384 | tf_op jit(solution)/shard_map/all_gather | solution.py:20
  106.6 3.7 %gather_fusion.1 = f32[16,64,128]{2,1,0:T(8,128)} fusion(f32[128,64,128]{2,1,0:T(8,128)} %bitcast.90, s32[1024]{0:T(1024)} %pad_clamp_fusion), kind=kCustom, calls=%fused_computation.1 | custom fusion | bytes 1048640 | tf_op jit(solution)/shard_map/gather | solution.py:151
  110.3 11.8 %all-gather.4.cloned.1.call-done = f32[2,1,32,64,128]{4,3,2,1,0:T(8,128)} async-done(((f32[1,1,32,64,128]{4,3,2,1,0:T(8,128)}), f32[2,1,32,64,128]{4,3,2,1,0:T(8,128)}) %all-gather.4.cloned.1.call-update) | async-done | bytes 2097168 | tf_op jit(solution)/shard_map/all_gather | solution.py:20
  123.0 26.2 %all-gather.6.cloned.1.call-done = f32[32,64,128]{2,1,0:T(8,128)} async-done(((f32[16,64,128]{2,1,0:T(8,128)}), f32[32,64,128]{2,1,0:T(8,128)}) %all-gather.6.cloned.1.call-update) | async-done | bytes 1048592 | tf_op jit(solution)/shard_map/all_gather | solution.py:157
  173.4 3.4 %fusion.9 = f32[1,128,2,16,64]{1,4,3,2,0:T(8,128)} fusion(f32[1,128,2,16,64]{1,4,3,2,0:T(8,128)} %fusion.17, bf16[128,2,16,64]{0,3,2,1:T(8,128)(2,1)} %bitcast.506, f32[2,16,128]{2,1,0:T(8,128)} %bitcast.550, f32[2,16,128]{2,1,0:T(8,128)} %copy.449, f32[2,128,128]{2,1,0:T(8,128)} %fusion.179, pred[128,128]{1,0:T(8,128)(4,1)} %iota_compare_fusion.2), kind=kOutput, calls=%fused_computation.50 | convolution fusion | flops 70516736 | bytes 2801664 | tf_op jit(solution)/shard_map/rgkts,rsgkp->rtgkp/dot_general | solution.py:110
  179.3 3.4 %fusion.10 = f32[1,128,2,16,64]{1,4,3,2,0:T(8,128)} fusion(f32[1,128,2,16,64]{1,4,3,2,0:T(8,128)} %fusion.18, bf16[128,2,16,64]{0,3,2,1:T(8,128)(2,1)} %bitcast.508, f32[2,16,128]{2,1,0:T(8,128)} %bitcast.548, f32[2,16,128]{2,1,0:T(8,128)} %copy.483, f32[2,128,128]{2,1,0:T(8,128)} %fusion.170, pred[128,128]{1,0:T(8,128)(4,1)} %iota_compare_fusion.2), kind=kOutput, calls=%fused_computation.51 | convolution fusion | flops 70516736 | bytes 2801664 | tf_op jit(solution)/shard_map/rgkts,rsgkp->rtgkp/dot_general | solution.py:110
  199.8 3.3 %fusion.11 = f32[1,128,2,16,64]{1,4,3,2,0:T(8,128)} fusion(f32[1,128,2,16,64]{1,4,3,2,0:T(8,128)} %fusion.19, bf16[128,2,16,64]{0,3,2,1:T(8,128)(2,1)} %bitcast.501, f32[2,16,128]{2,1,0:T(8,128)S(1)} %bitcast.542, f32[2,16,128]{2,1,0:T(8,128)S(1)} %copy-done.82, f32[2,128,128]{2,1,0:T(8,128)S(1)} %fusion.168, pred[128,128]{1,0:T(8,128)(4,1)S(1)} %copy-done.92), kind=kOutput, calls=%fused_computation.52 | convolution fusion | flops 70516736 | bytes 2801664 | tf_op jit(solution)/shard_map/rgkts,rsgkp->rtgkp/dot_general | solution.py:110
  203.1 2.6 copy.490
  205.8 7.2 %fusion.253 = (f32[1,128,2048]{2,1,0:T(8,128)}, f32[1,128,2048]{2,1,0:T(8,128)}, f32[1,128,2048]{2,1,0:T(8,128)}, f32[1,128,2048]{2,1,0:T(8,128)}, f32[1,128,204...) fusion(f32[1,128,2048]{2,1,0:T(8,128)S(1)} %copy.515, ...), kind=kLoop, calls=%fused_computation.411 | loop fusion | flops 14680064 | bytes 20971520 | tf_op jit(solution)/shard_map/mul | solution.py:178
  213.0 3.2 %mul.1454 = f32[128,2,1024]{2,1,0:T(2,128)} reshape(f32[1,128,2048]{2,1,0:T(8,128)} %get-tuple-element.56) | data formatting | bytes 2097152 | tf_op jit(solution)/shard_map/mul | solution.py:178
  219.1 3.2 %mul.1456 = f32[1,128,2048]{2,1,0:T(8,128)} reshape(f32[128,2,1024]{2,1,0:T(2,128)} %mul.1455) | data formatting | bytes 2097152 | tf_op jit(solution)/shard_map/mul | solution.py:180
  222.3 3.1 mul.1418
  228.3 3.1 %mul.1420 = f32[1,128,2048]{2,1,0:T(8,128)} reshape(f32[128,2,1024]{2,1,0:T(2,128)} %mul.1419) | data formatting | bytes 2097152 | tf_op jit(solution)/shard_map/mul | solution.py:180
  231.4 3.1 mul.1400
  237.4 3.1 %mul.1402 = f32[1,128,2048]{2,1,0:T(8,128)} reshape(f32[128,2,1024]{2,1,0:T(2,128)} %mul.1401) | data formatting | bytes 2097152 | tf_op jit(solution)/shard_map/mul | solution.py:180
  240.5 3.1 mul.1382
  246.5 3.1 %mul.1384 = f32[1,128,2048]{2,1,0:T(8,128)} reshape(f32[128,2,1024]{2,1,0:T(2,128)} %mul.1383) | data formatting | bytes 2097152 | tf_op jit(solution)/shard_map/mul | solution.py:180
  249.6 3.1 mul.1364
  255.8 3.1 %mul.1366 = f32[1,128,2048]{2,1,0:T(8,128)} reshape(f32[128,2,1024]{2,1,0:T(2,128)} %mul.1365) | data formatting | bytes 2097152 | tf_op jit(solution)/shard_map/mul | solution.py:180
  258.9 3.1 mul.1346
  264.9 3.1 mul.1348
  268.0 3.1 mul.1326
  274.0 3.1 %mul.1328 = f32[1,128,2048]{2,1,0:T(8,128)} reshape(f32[128,2,1024]{2,1,0:T(2,128)} %mul.1327) | data formatting | bytes 2097152 | tf_op jit(solution)/shard_map/mul | solution.py:180
  277.1 3.1 mul.1436
  283.1 3.2 %mul.1438 = f32[1,128,2048]{2,1,0:T(8,128)} reshape(f32[128,2,1024]{2,1,0:T(2,128)} %mul.1437) | data formatting | bytes 2097152 | tf_op jit(solution)/shard_map/mul | solution.py:180
  286.3 3.0 fusion.115
  289.3 2.7 fusion.116
  (410 shorter events, 142.0 us)
Async XLA Ops:
  7.2 8.6 %copy-start.103 = (s32[16,128]{1,0:T(8,128)S(1)}, s32[16,128]{1,0:T(8,128)}, u32[]{:S(2)}) copy-start(s32[16,128]{1,0:T(8,128)} %param.32) | copy-start | bytes 24580
  8.6 48.6 %collective-permute-start = (bf16[1,3,2048]{2,1,0:T(4,128)(2,1)}, bf16[1,3,2048]{2,1,0:T(4,128)(2,1)}, u32[]{:S(2)}, u32[]{:S(2)}) collective-permute-start(bf16[1,3,2048]{2,1,0:T(4,128)(2,1)} %slice.271), channel_id=1, source_target_pairs={{0,64},{1,65},{2,66},{3,67},{4,68},{5,69},{6,70},{7,71},{8,72},{9,... | collective-permute-start | bytes 36872 | tf_op jit(solution)/shard_map/ppermute | solution.py:15
  14.5 41.0 %collective-permute-start.1 = (bf16[1,3,2,256]{3,1,2,0:T(4,128)(2,1)S(1)}, bf16[1,3,2,256]{3,1,2,0:T(4,128)(2,1)S(1)}, u32[]{:S(2)}, u32[]{:S(2)}) collective-permute-start(bf16[1,3,2,256]{3,1,2,0:T(4,128)(2,1)S(1)} %slice.369), channel_id=1, source_target_pairs={{0,64},{1,65},{2,66},{3,67},{4,68},{5,69},{6,70},{7,71},{8,72},{9,... | collective-permute-start | bytes 9224 | tf_op jit(solution)/shard_map/ppermute | solution.py:15
  26.8 13.5 %copy-start.73 = (bf16[1,1024,32]{1,2,0:T(8,128)(2,1)S(1)}, bf16[1,1024,32]{1,2,0:T(8,128)(2,1)}, u32[]{:S(2)}) copy-start(bf16[1,1024,32]{1,2,0:T(8,128)(2,1)} %param.21) | copy-start | bytes 196612
  26.8 13.5 %copy-start.116 = (f32[32]{0:T(128)S(1)}, f32[32]{0:T(128)}, u32[]{:S(2)}) copy-start(f32[32]{0:T(128)} %param.28) | copy-start | bytes 388
  26.8 13.5 %copy-start.117 = (f32[32]{0:T(128)S(1)}, f32[32]{0:T(128)}, u32[]{:S(2)}) copy-start(f32[32]{0:T(128)} %param.29) | copy-start | bytes 388
  26.8 79.7 %all-to-all-start = ((f32[64,2,64,128]{3,2,1,0:T(8,128)}), f32[64,2,64,128]{3,2,1,0:T(8,128)}, u32[]{:S(2)}, u32[]{:S(2)}) async-start(f32[64,2,64,128]{3,2,1,0:T(8,128)} %broadcast_select_fusion), calls=%async_computation | async-start | bytes 8388608 | tf_op jit(solution)/shard_map/all_to_all | solution.py:148
  38.8 83.4 %all-gather.4.cloned.1.call-start = ((), (), s32[]{:S(2)}) async-start(), calls=%async_computation.1 | async-start | bytes 3145728 | tf_op jit(solution)/shard_map/all_gather | solution.py:20
  40.5 8.9 %copy-start.66 = (f32[1,128,32]{1,2,0:T(8,128)}, f32[1,128,32]{1,2,0:T(8,128)S(1)}, u32[]{:S(2)}) copy-start(f32[1,128,32]{1,2,0:T(8,128)S(1)} %get-tuple-element.83) | copy-start | bytes 49156
  40.5 9.6 %copy-start.65 = (f32[1,128,32]{1,2,0:T(8,128)}, f32[1,128,32]{1,2,0:T(8,128)S(1)}, u32[]{:S(2)}) copy-start(f32[1,128,32]{1,2,0:T(8,128)S(1)} %get-tuple-element.89) | copy-start | bytes 49156
  40.5 10.2 %copy-start.59 = (f32[1,128,32]{1,2,0:T(8,128)}, f32[1,128,32]{1,2,0:T(8,128)S(1)}, u32[]{:S(2)}) copy-start(f32[1,128,32]{1,2,0:T(8,128)S(1)} %get-tuple-element.88) | copy-start | bytes 49156
  40.6 10.9 %copy-start.67 = (f32[1,128,32]{1,2,0:T(8,128)}, f32[1,128,32]{1,2,0:T(8,128)S(1)}, u32[]{:S(2)}) copy-start(f32[1,128,32]{1,2,0:T(8,128)S(1)} %get-tuple-element.87) | copy-start | bytes 49156
  40.6 11.6 %copy-start.61 = (f32[1,128,32]{1,2,0:T(8,128)}, f32[1,128,32]{1,2,0:T(8,128)S(1)}, u32[]{:S(2)}) copy-start(f32[1,128,32]{1,2,0:T(8,128)S(1)} %get-tuple-element.86) | copy-start | bytes 49156
  40.6 12.3 %copy-start.69 = (f32[1,128,32]{1,2,0:T(8,128)}, f32[1,128,32]{1,2,0:T(8,128)S(1)}, u32[]{:S(2)}) copy-start(f32[1,128,32]{1,2,0:T(8,128)S(1)} %get-tuple-element.85) | copy-start | bytes 49156
  40.6 12.9 %copy-start.63 = (f32[1,128,32]{1,2,0:T(8,128)}, f32[1,128,32]{1,2,0:T(8,128)S(1)}, u32[]{:S(2)}) copy-start(f32[1,128,32]{1,2,0:T(8,128)S(1)} %get-tuple-element.84) | copy-start | bytes 49156
  40.6 13.6 %copy-start.71 = (f32[1,128,32]{1,2,0:T(8,128)}, f32[1,128,32]{1,2,0:T(8,128)S(1)}, u32[]{:S(2)}) copy-start(f32[1,128,32]{1,2,0:T(8,128)S(1)} %get-tuple-element.90) | copy-start | bytes 49156
  40.9 7.8 %copy-start.104 = (f32[4,2,256]{2,1,0:T(2,128)S(1)}, f32[4,2,256]{2,1,0:T(2,128)}, u32[]{:S(2)}) copy-start(f32[4,2,256]{2,1,0:T(2,128)} %param.26) | copy-start | bytes 24580
  40.9 7.8 %copy-start.74 = (f32[4,2048]{1,0:T(4,128)S(1)}, f32[4,2048]{1,0:T(4,128)}, u32[]{:S(2)}) copy-start(f32[4,2048]{1,0:T(4,128)} %param.24) | copy-start | bytes 98308
  42.4 13.1 %copy-start.106 = (bf16[1,3,2,256]{3,2,1,0:T(2,128)(2,1)S(1)}, bf16[1,3,2,256]{3,2,1,0:T(2,128)(2,1)}, u32[]{:S(2)}) copy-start(bf16[1,3,2,256]{3,2,1,0:T(2,128)(2,1)} %param.23) | copy-start | bytes 9220
  43.6 12.1 %copy-start.40 = (f32[1,128,2,16]{3,2,1,0:T(2,128)}, f32[1,128,2,16]{3,2,1,0:T(2,128)S(1)}, u32[]{:S(2)}) copy-start(f32[1,128,2,16]{3,2,1,0:T(2,128)S(1)} %fusion.270) | copy-start | bytes 49156
  44.6 11.1 %copy-start.41 = (f32[1,128,2,16]{3,2,1,0:T(2,128)}, f32[1,128,2,16]{3,2,1,0:T(2,128)S(1)}, u32[]{:S(2)}) copy-start(f32[1,128,2,16]{3,2,1,0:T(2,128)S(1)} %fusion.271) | copy-start | bytes 49156
  45.6 10.2 %copy-start.42 = (f32[1,128,2,16]{3,2,1,0:T(2,128)}, f32[1,128,2,16]{3,2,1,0:T(2,128)S(1)}, u32[]{:S(2)}) copy-start(f32[1,128,2,16]{3,2,1,0:T(2,128)S(1)} %fusion.272) | copy-start | bytes 49156
  46.5 9.3 %copy-start.43 = (f32[1,128,2,16]{3,2,1,0:T(2,128)}, f32[1,128,2,16]{3,2,1,0:T(2,128)S(1)}, u32[]{:S(2)}) copy-start(f32[1,128,2,16]{3,2,1,0:T(2,128)S(1)} %fusion.273) | copy-start | bytes 49156
  47.4 9.8 %copy-start.44 = (f32[1,128,2,16]{3,2,1,0:T(2,128)}, f32[1,128,2,16]{3,2,1,0:T(2,128)S(1)}, u32[]{:S(2)}) copy-start(f32[1,128,2,16]{3,2,1,0:T(2,128)S(1)} %fusion.266) | copy-start | bytes 49156
  47.4 8.3 %copy-start.107 = (f32[2,256]{1,0:T(2,128)S(1)}, f32[2,256]{1,0:T(2,128)}, u32[]{:S(2)}) copy-start(f32[2,256]{1,0:T(2,128)} %param.27) | copy-start | bytes 6148
  57.2 48.6 %copy-start.5 = (bf16[1,1024,2,256]{3,1,2,0:T(8,128)(2,1)}, bf16[1,1024,2,256]{3,1,2,0:T(8,128)(2,1)S(1)}, u32[]{:S(2)}) copy-start(bf16[1,1024,2,256]{3,1,2,0:T(8,128)(2,1)S(1)} %multiply_convert_fusion.9) | copy-start | bytes 3145732
  66.5 8.4 %copy-start.39 = (bf16[1,128,2048]{2,1,0:T(8,128)(2,1)S(1)}, bf16[1,128,2048]{2,1,0:T(8,128)(2,1)}, u32[]{:S(2)}) copy-start(bf16[1,128,2048]{2,1,0:T(8,128)(2,1)} %get-tuple-element.68) | copy-start | bytes 1572868
  68.6 7.3 %copy-start.38 = (bf16[1,128,2048]{2,1,0:T(8,128)(2,1)S(1)}, bf16[1,128,2048]{2,1,0:T(8,128)(2,1)}, u32[]{:S(2)}) copy-start(bf16[1,128,2048]{2,1,0:T(8,128)(2,1)} %get-tuple-element.69) | copy-start | bytes 1572868
  70.7 6.2 %copy-start.37 = (bf16[1,128,2048]{2,1,0:T(8,128)(2,1)S(1)}, bf16[1,128,2048]{2,1,0:T(8,128)(2,1)}, u32[]{:S(2)}) copy-start(bf16[1,128,2048]{2,1,0:T(8,128)(2,1)} %get-tuple-element.70) | copy-start | bytes 1572868
  85.3 63.9 %all-gather.6.cloned.1.call-start = ((), (), s32[]{:S(2)}) async-start(), calls=%async_computation.3 | async-start | bytes 1572864 | tf_op jit(solution)/shard_map/all_gather | solution.py:157
  110.3 191.3 %all-reduce.2.cloned.1.call-start = ((), (), s32[]{:S(2)}) async-start(), calls=%async_computation.2 | async-start | bytes 2097152 | tf_op jit(solution)/shard_map/psum | solution.py:33
  280.2 6.1 %copy-start.115 = (f32[128]{0:T(128)S(1)}, f32[128]{0:T(128)}, u32[]{:S(2)}) copy-start(f32[128]{0:T(128)} %get-tuple-element.132) | copy-start | bytes 1540
  (92 other events, 209.9 us)
Sparse Core Ops, SparseCore 0:
  85.4 36.7 all-gather.3
  124.4 24.7 all-gather.5
  185.3 47.5 all-reduce.1
where the time goes:
time: 316 us; the launch traced here: 310 us
  local copies, waits for them, and re-layouts  126 us (40%)
  other arithmetic  62.7 us (20%)
  matrix products  45.1 us (14%)
  waiting for transfers between devices  38 us (12%)
  starting transfers between devices  18.1 us (6%)
  between operations  16.2 us (5%)
  blocking collectives  3.46 us (1%)
    mul x16, local copies, waits for them, and re-layouts, body(): grouped * inverse_rms  35.7 us
    all_gather x1, waiting for transfers between devices, body(): start_all = lax.all_gather(start_quarter, 'section', axis=1, tiled=True)  26.2 us
    mul x8, local copies, waits for them, and re-layouts, body(): grouped * grouped  24.7 us
    dot_general x8, matrix products, body(): jnp.einsum('rgkts,rsgkp->rtgkp', weights, x_block, preferred_element_type...  19.7 us
    reshape x8, local copies, waits for them, and re-layouts, body(): y_all.reshape(requests, BLK, channels)  17.5 us
    dot_general x8, matrix products, body(): jnp.einsum('rtgn,rgkpn->rtgkp', c_block, carried.astype(jnp.bfloat16), pr...  14.7 us
    slice x9, local copies, waits for them, and re-layouts, body(): x_conv[:, window].reshape(requests, BLK, group_count, per_group, head_dim)  13.5 us
    unnamed x7, other arithmetic  13 us
  transfers between devices with their start and end apart: 6, of which 2 were waited for; matrix products, arithmetic and copies ran while one was open for 62% of the time, Pallas kernels for 0%

commit v1 on v0

v1 whole, which is shorter than its diff:
```python
import functools

import jax
import jax.numpy as jnp
from jax import lax
from jax.experimental import pallas as pl
from jax.experimental.pallas import tpu as pltpu
from jax.sharding import PartitionSpec as P

BLK = 128
EPS = 1e-05
MIB = 1 << 20
F32 = jnp.float32
BF16 = jnp.bfloat16
SMEM = pltpu.SMEM
VMEM = pltpu.VMEM


def dot(a, b):
    return jnp.dot(a, b, preferred_element_type=F32)


def silu(v):
    half = 0.5 * v
    return half * jnp.tanh(half) + half


def split_two(v):
    high = v.astype(BF16)
    return high, (v - high.astype(F32)).astype(BF16)


def split_three(v):
    high = v.astype(BF16)
    rest = v - high.astype(F32)
    mid = rest.astype(BF16)
    return high, mid, (rest - mid.astype(F32)).astype(BF16)


def iota(shape, dim):
    return lax.broadcasted_iota(jnp.int32, shape, dim)


def pack_kernel(picked_ref, pool_ref, out_ref):
    count = out_ref.shape[0]
    first = pl.program_id(0) * count

    def one(i, carry):
        out_ref[i] = pool_ref[picked_ref[first + i]].astype(BF16)
        return carry

    lax.fori_loop(0, count, one, 0, unroll=8)


def pack(picked, pool):
    count = picked.shape[0]
    steps = 8
    rows = count // steps
    return pl.pallas_call(
        pack_kernel,
        out_shape=jax.ShapeDtypeStruct((count,) + pool.shape[1:], BF16),
        grid=(steps,),
        in_specs=[
            pl.BlockSpec(memory_space=SMEM),
            pl.BlockSpec(pool.shape, lambda i: (0, 0, 0)),
        ],
        out_specs=pl.BlockSpec((rows,) + pool.shape[1:], lambda i: (i, 0, 0)),
        compiler_params=pltpu.CompilerParams(vmem_limit_bytes=16 * MIB),
        cost_estimate=pl.CostEstimate(flops=0, bytes_accessed=6 * MIB, transcendentals=0),
        name="pack_states",
    )(picked, pool)


def select_kernel(index_ref, incoming_ref, out_ref):
    for pair in range(out_ref.shape[1] // BLK):
        two = jnp.concatenate(
            [incoming_ref[index_ref[2 * pair + k]].astype(F32) for k in range(2)], 0
        )
        out_ref[:, pair * BLK : (pair + 1) * BLK] = two.T.astype(BF16)


def select(index, incoming):
    heads = index.shape[0]
    _, head_dim, state_size = incoming.shape
    return pl.pallas_call(
        select_kernel,
        out_shape=jax.ShapeDtypeStruct((state_size, heads * head_dim), BF16),
        in_specs=[pl.BlockSpec(memory_space=SMEM), pl.BlockSpec(memory_space=VMEM)],
        out_specs=pl.BlockSpec(memory_space=VMEM),
        compiler_params=pltpu.CompilerParams(vmem_limit_bytes=16 * MIB),
        cost_estimate=pl.CostEstimate(flops=0, bytes_accessed=3 * MIB, transcendentals=0),
        name="select_states",
    )(index, incoming)


def local_kernel(
    place_ref, x_ref, z_ref, bc_ref, dt_ref, step_ref, halo_ref, taps_ref,
    a_ref, b_ref, c_ref, t_ref,
    spread, factors, behind, state, decay,
    *, groups, blocks, head_dim, head_count,
):
    step = pl.program_id(0)
    channels = x_ref.shape[1]
    width = channels // groups
    lanes = dt_ref.shape[1]
    halves = lanes // BLK
    chunk = 256

    @pl.when(step == 0)
    def _():
        behind[...] = halo_ref[...]
        state[...] = jnp.zeros_like(state)
        decay[...] = jnp.ones_like(decay)
        for at in range(0, channels, BLK):
            shape = (spread.shape[0], BLK)
            head = lax.div(iota(shape, 1) + at, head_dim)
            spread[:, at : at + BLK] = jnp.where(
                (iota(shape, 0) & (head_count - 1)) == head, 1.0, 0.0
            ).astype(BF16)
        value = dt_ref[...].astype(F32) + step_ref[0:1, :]
        soft = jnp.maximum(value, 0.0) + jnp.log1p(jnp.exp(-jnp.abs(value)))
        shape = (BLK, lanes)
        position = place_ref[1] + lax.div(iota(shape, 1), head_count) * BLK + iota(shape, 0)
        steps = jnp.where(position < place_ref[0], soft, 0.0)
        log_decay = -steps * step_ref[1:2, :]
        lower = jnp.where(iota((BLK, BLK), 0) >= iota((BLK, BLK), 1), 1.0, 0.0).astype(BF16)
        cum_log = sum(dot(lower, part) for part in split_three(log_decay))
        both = (jnp.exp(cum_log), steps * jnp.exp(-cum_log))
        for row, full in enumerate(both):
            for part, values in enumerate(split_two(full)):
                for block in range(blocks):
                    per = BLK // head_count
                    piece = values[:, block // per * BLK : (block // per + 1) * BLK].astype(F32)
                    owner = lax.div(iota((BLK, BLK), 1), head_count)
                    factors[
                        block, row * BLK : (row + 1) * BLK, part * BLK : (part + 1) * BLK
                    ] = jnp.where(owner == block % per, piece, 0.0).astype(BF16)

    def conv(source, at, size, base):
        now = source[:, at : at + size].astype(F32)
        cols = slice(base + at, base + at + size)
        joined = jnp.concatenate([behind[:, cols], now], 0)
        total = taps_ref[4:5, cols] + taps_ref[3:4, cols] * now
        for k in range(3):
            total = total + taps_ref[k : k + 1, cols] * joined[5 + k : 5 + k + BLK]
        behind[:, cols] = now[BLK - 8 :]
        return silu(total)

    causal = iota((BLK, BLK), 0) >= iota((BLK, BLK), 1)
    for group in range(groups):
        mixed = conv(bc_ref, group * 2 * BLK, 2 * BLK, channels)
        b_block = mixed[:, :BLK]
        c_block = mixed[:, BLK:].astype(BF16)
        b_turned = b_block.T.astype(BF16)
        c_ref[:, group * BLK : (group + 1) * BLK] = c_block
        scores = jnp.where(causal, dot(c_block, b_turned), 0.0).astype(BF16)
        left = jnp.concatenate([scores, c_block], 1)
        for at in range(group * width, (group + 1) * width, chunk):
            cols = slice(at, at + chunk)
            x_conv = conv(x_ref, at, chunk, 0)
            scale = dot(factors[step], spread[:, cols])
            risen = scale[:BLK]
            inner = (x_conv * scale[BLK:]).astype(BF16)
            before = state[:, cols]
            y_local = risen * dot(left, jnp.concatenate([inner, before.astype(BF16)], 0))
            last = risen[BLK - 1 :]
            state[:, cols] = last * (before + dot(b_turned, inner))
            gate = silu(z_ref[:, cols].astype(F32))
            passed = decay[0:1, cols]
            a_ref[:, cols] = (y_local * gate).astype(BF16)
            b_ref[:, cols] = (risen * passed * gate).astype(BF16)
            decay[0:1, cols] = passed * last

    @pl.when(step == blocks - 1)
    def _():
        t_ref[:BLK] = state[...].astype(BF16)
        parts = split_three(decay[0:1, :])
        row = iota((16, channels), 0)
        stacked = jnp.zeros((16, channels), F32)
        for k, part in enumerate(parts):
            stacked = jnp.where(row == k, part.astype(F32), stacked)
        t_ref[BLK:] = stacked.astype(BF16)


def local_part(place, x, z, bc, dt, step_rows, halo, taps, groups, head_count):
    seg_len, channels = x.shape
    blocks = seg_len // BLK
    body = functools.partial(
        local_kernel, groups=groups, blocks=blocks,
        head_dim=channels // head_count, head_count=head_count,
    )
    by_block = lambda width: pl.BlockSpec((BLK, width), lambda i: (i, 0))
    whole = lambda shape: pl.BlockSpec(shape, lambda i: (0,) * len(shape))
    return pl.pallas_call(
        body,
        out_shape=(
            jax.ShapeDtypeStruct((seg_len, channels), BF16),
            jax.ShapeDtypeStruct((seg_len, channels), BF16),
            jax.ShapeDtypeStruct((seg_len, groups * BLK), BF16),
            jax.ShapeDtypeStruct((BLK + 16, channels), BF16),
        ),
        grid=(blocks,),
        in_specs=[
            pl.BlockSpec(memory_space=SMEM),
            by_block(channels), by_block(channels), by_block(bc.shape[1]),
            whole(dt.shape), whole(step_rows.shape), whole(halo.shape), whole(taps.shape),
        ],
        out_specs=(
            by_block(channels), by_block(channels), by_block(groups * BLK),
            whole((BLK + 16, channels)),
        ),
        scratch_shapes=[
            VMEM((2 * BLK, channels), BF16),
            VMEM((blocks, 2 * BLK, 2 * BLK), BF16),
            VMEM(halo.shape, F32),
            VMEM((BLK, channels), F32),
            VMEM((8, channels), F32),
        ],
        compiler_params=pltpu.CompilerParams(vmem_limit_bytes=32 * MIB),
        cost_estimate=pl.CostEstimate(
            flops=2 * seg_len * channels * 1024, bytes_accessed=20 * MIB,
            transcendentals=2 * seg_len * channels,
        ),
        name="local_blocks",
    )(place, x, z, bc, dt, step_rows, halo, taps)


def join_kernel(
    place_ref, a_ref, b_ref, c_ref, own_ref, other_ref, mine_ref, theirs_ref, gain_ref,
    out_ref, final_ref,
    start, gated,
    *, groups,
):
    step = pl.program_id(0)
    section = place_ref[2]
    width = a_ref.shape[1] // groups
    chunk = 256

    def decay_of(ref, cols):
        rows = ref[BLK : BLK + 16, cols].astype(F32)
        return rows[0:1] + rows[1:2] + rows[2:3]

    @pl.when(step == 0)
    def _():
        for group in range(groups):
            for at in range(0, width, BLK):
                cols = slice(group * width + at, group * width + at + BLK)
                here = slice(at, at + BLK)

                def moved(first, second, cached):
                    middle = decay_of(first, cols) * cached + first[:BLK, cols].astype(F32)
                    return middle, decay_of(second, cols) * middle + second[:BLK, cols].astype(F32)

                @pl.when(section == 0)
                def _():
                    if group == 0:
                        cached = own_ref[:, here].astype(F32)
                        final_ref[here, :] = moved(mine_ref, theirs_ref, cached)[1].T
                        start[:, cols] = own_ref[:, here]
                    else:
                        start[:, cols] = other_ref[:, here]

                @pl.when(section == 1)
                def _():
                    source = own_ref if group == 1 else other_ref
                    middle, end = moved(theirs_ref, mine_ref, source[:, here].astype(F32))
                    start[:, cols] = middle.astype(BF16)
                    if group == 1:
                        final_ref[here, :] = end.T

    position = place_ref[1] + step * BLK + iota((BLK, 1), 0)
    live = (position < place_ref[0]).astype(F32)
    for group in range(groups):
        c_block = c_ref[:, group * BLK : (group + 1) * BLK]
        squares = jnp.zeros((BLK, BLK), F32)
        for at in range(0, width, chunk):
            cols = slice(group * width + at, group * width + at + chunk)
            inter = dot(c_block, start[:, cols])
            value = a_ref[:, cols].astype(F32) + b_ref[:, cols].astype(F32) * inter
            gated[:, at : at + chunk] = value
            square = value * value
            for k in range(chunk // BLK):
                squares = squares + square[:, k * BLK : (k + 1) * BLK]
        mean = jnp.sum(squares, 1, keepdims=True) * (1.0 / width)
        scale = lax.rsqrt(mean + EPS) * live
        for at in range(0, width, chunk):
            cols = slice(group * width + at, group * width + at + chunk)
            out_ref[:, cols] = (
                gated[:, at : at + chunk] * scale * gain_ref[0:1, cols]
            ).astype(BF16)


def join_part(place, a, b, c, own, other, mine, theirs, gain, groups):
    seg_len, channels = a.shape
    by_block = lambda width: pl.BlockSpec((BLK, width), lambda i: (i, 0))
    whole = lambda shape: pl.BlockSpec(shape, lambda i: (0,) * len(shape))
    final_shape = (own.shape[1], own.shape[0])
    return pl.pallas_call(
        functools.partial(join_kernel, groups=groups),
        out_shape=(
            jax.ShapeDtypeStruct((seg_len, channels), BF16),
            jax.ShapeDtypeStruct(final_shape, F32),
        ),
        grid=(seg_len // BLK,),
        in_specs=[
            pl.BlockSpec(memory_space=SMEM),
            by_block(channels), by_block(channels), by_block(c.shape[1]),
            whole(own.shape), whole(other.shape), whole(mine.shape), whole(theirs.shape),
            whole(gain.shape),
        ],
        out_specs=(by_block(channels), whole(final_shape)),
        scratch_shapes=[VMEM((BLK, channels), BF16), VMEM((BLK, channels // groups), F32)],
        compiler_params=pltpu.CompilerParams(vmem_limit_bytes=32 * MIB),
        cost_estimate=pl.CostEstimate(
            flops=2 * seg_len * channels * BLK, bytes_accessed=16 * MIB, transcendentals=0
        ),
        name="join_blocks",
    )(place, a, b, c, own, other, mine, theirs, gain)


def body(
    x_in,
    z_in,
    bc_in,
    dt_in,
    tail_x,
    tail_bc,
    conv_w_x,
    conv_b_x,
    conv_w_bc,
    conv_b_bc,
    dt_bias,
    decay_rate,
    norm_gain,
    state_pool,
    block_slots,
    new_len,
):
    section = lax.axis_index("section")
    section_count = lax.axis_size("section")
    cache_count = lax.axis_size("cache")
    mp_count = lax.axis_size("mp")
    peer_count = cache_count * mp_count
    peer_self = lax.axis_index("cache") * mp_count + lax.axis_index("mp")
    _, seg_len, channels = x_in.shape
    groups = bc_in.shape[2]
    state_size = bc_in.shape[3] // 2
    head_count = dt_in.shape[2]
    head_dim = channels // head_count
    quarter = head_count // section_count
    blocks = seg_len // BLK
    slots_dev = state_pool.shape[0]
    most_held = slots_dev // peer_count
    swap = [(0, 1), (1, 0)]

    listed = block_slots.reshape(cache_count, mp_count, section_count, quarter)
    listed = lax.dynamic_index_in_dim(listed, section, 2, keepdims=False)
    listed = listed.reshape(peer_count, quarter)
    owner = listed // slots_dev % peer_count
    key = jnp.arange(quarter, dtype=jnp.int32)[None, :] * slots_dev + listed % slots_dev
    mine = owner == peer_self
    first = jnp.min(jnp.where(mine, key, quarter * slots_dev), 1) % slots_dev
    last = jnp.max(jnp.where(mine, key, 0), 1) % slots_dev
    picked = jnp.stack([first, last], 1).reshape(peer_count * most_held)
    outgoing = pack(picked, state_pool)
    incoming = lax.all_to_all(
        outgoing.reshape(peer_count, most_held * head_dim, state_size),
        ("cache", "mp"), split_axis=0, concat_axis=0, tiled=True,
    )
    own_owner = lax.dynamic_index_in_dim(owner, peer_self, 0, keepdims=False)
    order = jnp.arange(quarter)
    again = (own_owner[:, None] == own_owner[None, :]) & (order[None, :] < order[:, None])
    index = own_owner * most_held + jnp.any(again, 1).astype(jnp.int32)

    x2, z2, dt2 = x_in[0], z_in[0], dt_in[0]
    bc2 = bc_in[0].reshape(seg_len, groups * 2 * state_size)
    edge = jnp.concatenate(
        [x2[seg_len - 16 :], bc_in[0, seg_len - 16 :].reshape(16, groups * 2 * state_size)], 1
    )
    received = lax.ppermute(edge, "section", [(0, 1)])
    tail = jnp.concatenate([tail_x[0], tail_bc[0].reshape(3, groups * 2 * state_size)], 1)
    halo = jnp.where(section == 0, jnp.pad(tail, ((5, 0), (0, 0))), received[8:]).astype(F32)

    dt_rows = dt2.reshape(blocks, BLK, head_count).transpose(1, 0, 2).reshape(BLK, -1)
    step_rows = jnp.tile(jnp.stack([dt_bias, decay_rate]), (1, blocks))
    taps = jnp.concatenate(
        [
            jnp.concatenate([conv_w_x, conv_w_bc.reshape(4, -1)], 1),
            jnp.concatenate([conv_b_x, conv_b_bc.reshape(-1)])[None],
        ],
        0,
    )
    place = jnp.stack(
        [new_len[0], section.astype(jnp.int32) * seg_len, section.astype(jnp.int32)]
    )
    a, b, c, summary = local_part(
        place, x2, z2, bc2, dt_rows, step_rows, halo, taps, groups, head_count
    )
    theirs = lax.ppermute(summary, "section", swap)

    own = select(index, incoming.reshape(peer_count * most_held, head_dim, state_size))
    other = lax.ppermute(own, "section", swap)
    gated, final = join_part(
        place, a, b, c, own, other, summary, theirs, norm_gain[None], groups
    )
    return (
        gated[None],
        final.reshape(1, 1, 1, quarter, head_dim, state_size),
    )


def solution(mesh):
    in_specs = (
        P("cache", "section", "mp"),
        P("cache", "section", "mp"),
        P("cache", "section", "mp", None),
        P("cache", "section", "mp"),
        P("cache", None, "mp"),
        P("cache", None, "mp", None),
        P(None, "mp"),
        P("mp"),
        P(None, "mp", None),
        P("mp", None),
        P("mp"),
        P("mp"),
        P("mp"),
        P(("section", "cache", "mp"), None, None),
        P(),
        P("cache"),
    )
    out_specs = (P("cache", "section", "mp"), P("cache", "mp", "section", None, None, None))
    return jax.shard_map(body, mesh=mesh, in_specs=in_specs, out_specs=out_specs, check_vma=False)
```

time: 316 us -> 90.2 us (0.29)
  the two profiles are of different devices: /device:TPU:1 before, /device:TPU:6 now
where the time goes in v1:
time: 90.2 us; the launch traced here: 88.5 us
  Pallas kernels  28.4 us (31%)
  local copies, waits for them, and re-layouts  21.3 us (24%)
  waiting for transfers between devices  18.5 us (21%)
  starting transfers between devices  15.6 us (17%)
  other arithmetic  3.08 us (3%)
  between operations  1.63 us (2%)
    unnamed x44, local copies, waits for them, and re-layouts  18.2 us
    pallas_call x1, Pallas kernels, local_part(): pl.pallas_call(body, out_shape=(jax.ShapeDtypeStruct((seg_len, channels),...  16.2 us
    ppermute x1, waiting for transfers between devices, body(): theirs = lax.ppermute(summary, 'section', swap)  13.3 us
    all_to_all x1, starting transfers between devices, body(): lax.all_to_all(outgoing.reshape(peer_count, most_held * head_dim, state_s...  11.6 us
    pallas_call x1, Pallas kernels, join_part(): pl.pallas_call(functools.partial(join_kernel, groups=groups), out_shape=(...  7.81 us
    ppermute x1, waiting for transfers between devices, body(): other = lax.ppermute(own, 'section', swap)  5.15 us
    pallas_call x1, Pallas kernels, pack(): pl.pallas_call(pack_kernel, out_shape=jax.ShapeDtypeStruct((count,) + poo...  3.72 us
    ppermute x1, starting transfers between devices, body(): theirs = lax.ppermute(summary, 'section', swap)  2.64 us
  transfers between devices with their start and end apart: 4, of which 2 were waited for; matrix products, arithmetic and copies ran while one was open for 7% of the time, Pallas kernels for 23%

profile of v1, /device:TPU:6, one launch (start us, length us, event | category | flops | bytes accessed | tf_op | source)
XLA Modules:
  0.0 88.5 jit_solution(18373768660415891130)
XLA Ops:
  0.6 0.7 slice.14
  1.4 0.8 slice_bitcast_fusion
  2.2 1.3 %collective-permute-start = (bf16[16,2560]{1,0:T(8,128)(2,1)S(1)}, bf16[16,2560]{1,0:T(8,128)(2,1)S(1)}, u32[]{:S(2)}, u32[]{:S(2)}) collective-permute-start(bf16[16,2560]{1,0:T(8,128)(2,1)S(1)} %pad_maximum_fusion), channel_id=1, source_target_pairs={{0,64},{1,65},{2,66},{3,67},{4,68},{5,69},{6,70},{7,71},{8,72},{9,... | collective-permute-start | bytes 245768 | tf_op jit(solution)/shard_map/ppermute | solution.py:380
  3.6 0.8 reshape.167
  4.4 0.3 and_select_fusion.1
  4.7 2.4 %fusion.8 = (s32[16,4]{1,0:T(8,128)S(1)}, s32[16,4]{1,0:T(8,128)S(1)}) fusion(s32[16,4,1,16]{3,2,1,0:T(1,128)S(1)} %get-tuple-element.16, s32[]{:T(128)S(6)} %add.71, s32[16,4,1,16]{3,2,1,0:T(1,128)S(1)} %get-tuple-element.17, s32[16]{0:T(128)S(1)} %iota_multiply_fusion), kind=kLoop, calls=%fused_computation.28 | loop fusion | flops 11136 | bytes 8772 | tf_op jit(solution)/shard_map/reduce_min | solution.py:362
  7.0 0.1 reduce_min.12
  7.1 0.1 reduce_max.12
  7.3 0.1 copy.27
  7.4 0.1 reshape.169.picked_ref
  7.5 2.2 %copy-done = f32[128,64,128]{2,1,0:T(8,128)S(1)} copy-done((f32[128,64,128]{2,1,0:T(8,128)S(1)}, f32[128,64,128]{2,1,0:T(8,128)}, u32[]{:S(2)}) %copy-start) | copy-done | bytes 4194328
  9.7 3.7 %pack_states.1 = bf16[128,64,128]{2,1,0:T(8,128)(2,1)} custom-call(s32[128]{0:T(128)S(1)} %reshape.169.picked_ref, f32[128,64,128]{2,1,0:T(8,128)S(1)} %copy-done), custom_call_target="tpu_custom_call" | custom-call | bytes 6291456 | tf_op jit(solution)/shard_map/pack_states/pallas_call | solution.py:59
  13.5 11.6 %all-to-all-start = ((bf16[64,128,128]{2,1,0:T(8,128)(2,1)}), bf16[64,128,128]{2,1,0:T(8,128)(2,1)S(1)}, u32[]{:S(2)}, u32[]{:S(2)}) async-start(bf16[64,128,128]{2,1,0:T(8,128)(2,1)} %bitcast.12), calls=%async_computation | async-start | bytes 4194304 | tf_op jit(solution)/shard_map/all_to_all | solution.py:366
  26.0 0.1 copy.26.dt_ref
  26.1 1.5 %copy.28 = bf16[128,8,2,256]{3,1,2,0:T(8,128)(2,1)S(1)} copy(bf16[128,8,2,256]{3,2,1,0:T(2,128)(2,1)} %bitcast.43) | data formatting | bytes 2097152
  27.6 0.1 pad_add_fusion.1.place_ref
  27.8 2.2 %copy-done.8 = bf16[1,1024,2048]{2,1,0:T(8,128)(2,1)S(1)} copy-done((bf16[1,1024,2048]{2,1,0:T(8,128)(2,1)S(1)}, bf16[1,1024,2048]{2,1,0:T(8,128)(2,1)}, u32[]{:S(2)}) %copy-start.8) | copy-done | bytes 4194328
  30.0 2.2 %copy-done.9 = bf16[1,1024,2048]{2,1,0:T(8,128)(2,1)S(1)} copy-done((bf16[1,1024,2048]{2,1,0:T(8,128)(2,1)S(1)}, bf16[1,1024,2048]{2,1,0:T(8,128)(2,1)}, u32[]{:S(2)}) %copy-start.9) | copy-done | bytes 4194328
  32.2 16.2 %local_blocks.1 = (bf16[1024,2048]{1,0:T(8,128)(2,1)S(1)}, bf16[1024,2048]{1,0:T(8,128)(2,1)S(1)}, bf16[1024,256]{1,0:T(8,128)(2,1)S(1)}, bf16[144,2048]{1,0:T(8,128)(2,1)}) custom-call(s32[3]{0:T(128)S(1)} %pad_add_fusion.1.place_ref, bf16[1024,2048]{1,0:T(8,128)(2,1)S(1)} %bitcast.41, bf16[1024,2048]{1,0:T(8,128)(2,1)S(1)} %bitcast.42, ...), custom_call_target="tpu_custom_call" | custom-call | flops 4294967296 | bytes 20971520 | tf_op jit(solution)/shard_map/local_blocks/pallas_call | solution.py:194
  48.4 2.0 %copy-done.1 = bf16[1024,2048]{1,0:T(8,128)(2,1)} copy-done((bf16[1024,2048]{1,0:T(8,128)(2,1)}, bf16[1024,2048]{1,0:T(8,128)(2,1)S(1)}, u32[]{:S(2)}) %copy-start.1) | copy-done | bytes 4194328
  50.5 1.9 %copy-done.3 = bf16[1024,2048]{1,0:T(8,128)(2,1)} copy-done((bf16[1024,2048]{1,0:T(8,128)(2,1)}, bf16[1024,2048]{1,0:T(8,128)(2,1)S(1)}, u32[]{:S(2)}) %copy-start.3) | copy-done | bytes 4194328
  52.4 0.8 copy-done.5
  53.2 2.6 %collective-permute-start.2 = (bf16[144,2048]{1,0:T(8,128)(2,1)}, bf16[144,2048]{1,0:T(8,128)(2,1)S(1)}, u32[]{:S(2)}, u32[]{:S(2)}) collective-permute-start(bf16[144,2048]{1,0:T(8,128)(2,1)} %get-tuple-element.11.mine_ref), channel_id=1, source_target_pairs={{0,64},{64,0},{1,65},{65,1},{2,66},{66,2},{3,67},{67,3},{4,68},{68... | collective-permute-start | bytes 1769480 | tf_op jit(solution)/shard_map/ppermute | solution.py:399
  55.8 0.2 fusion.12
  56.0 0.7 select_states.1.own_ref
  56.7 0.1 collective-permute-start.1
  56.8 13.3 %collective-permute-done.2.theirs_ref = bf16[144,2048]{1,0:T(8,128)(2,1)S(1)} collective-permute-done((bf16[144,2048]{1,0:T(8,128)(2,1)}, bf16[144,2048]{1,0:T(8,128)(2,1)S(1)}, u32[]{:S(2)}, u32[]{:S(2)}) %collective-permute-start.2) | collective-permute-done | bytes 589856 | tf_op jit(solution)/shard_map/ppermute | solution.py:399
  70.2 5.1 %collective-permute-done.1.other_ref = bf16[128,1024]{1,0:T(8,128)(2,1)S(1)} collective-permute-done((bf16[128,1024]{1,0:T(8,128)(2,1)S(1)}, bf16[128,1024]{1,0:T(8,128)(2,1)S(1)}, u32[]{:S(2)}, u32[]{:S(2)}) %collective-permute-start.1) | collective-permute-done | bytes 262176 | tf_op jit(solution)/shard_map/ppermute | solution.py:402
  75.3 2.2 %copy-done.2 = bf16[1024,2048]{1,0:T(8,128)(2,1)S(1)} copy-done((bf16[1024,2048]{1,0:T(8,128)(2,1)S(1)}, bf16[1024,2048]{1,0:T(8,128)(2,1)}, u32[]{:S(2)}) %copy-start.2) | copy-done | bytes 4194328
  77.5 2.2 %copy-done.4 = bf16[1024,2048]{1,0:T(8,128)(2,1)S(1)} copy-done((bf16[1024,2048]{1,0:T(8,128)(2,1)S(1)}, bf16[1024,2048]{1,0:T(8,128)(2,1)}, u32[]{:S(2)}) %copy-start.4) | copy-done | bytes 4194328
  79.7 1.0 %copy-done.6 = bf16[1024,256]{1,0:T(8,128)(2,1)S(1)} copy-done((bf16[1024,256]{1,0:T(8,128)(2,1)S(1)}, bf16[1024,256]{1,0:T(8,128)(2,1)}, u32[]{:S(2)}) %copy-start.6) | copy-done | bytes 524312
  80.7 7.8 %join_blocks.1 = (bf16[1024,2048]{1,0:T(8,128)(2,1)}, f32[1024,128]{1,0:T(8,128)}) custom-call(s32[3]{0:T(128)S(1)} %pad_add_fusion.1.place_ref, bf16[1024,2048]{1,0:T(8,128)(2,1)S(1)} %copy-done.2, bf16[1024,2048]{1,0:T(8,128)(2,1)S(1)} %copy-done.4, bf16[1024,256]{1,0:T(8,128)(2,1)S(1)} %copy-done.6, bf16[128,1024]{1,0:T(8,128)(2,1)S(1)} %select_states.1.own_ref, ...), custom_call_target="tpu_custom_call" | custom-call | flops 536870912 | bytes 16777216 | tf_op jit(solution)/shard_map/join_blocks/pallas_call | solution.py:298
  (52 shorter events, 0.4 us)
Async XLA Ops:
  2.2 25.5 %collective-permute-start = (bf16[16,2560]{1,0:T(8,128)(2,1)S(1)}, bf16[16,2560]{1,0:T(8,128)(2,1)S(1)}, u32[]{:S(2)}, u32[]{:S(2)}) collective-permute-start(bf16[16,2560]{1,0:T(8,128)(2,1)S(1)} %pad_maximum_fusion), channel_id=1, source_target_pairs={{0,64},{1,65},{2,66},{3,67},{4,68},{5,69},{6,70},{7,71},{8,72},{9,... | collective-permute-start | bytes 245768 | tf_op jit(solution)/shard_map/ppermute | solution.py:380
  7.5 2.2 %copy-start = (f32[128,64,128]{2,1,0:T(8,128)S(1)}, f32[128,64,128]{2,1,0:T(8,128)}, u32[]{:S(2)}) copy-start(f32[128,64,128]{2,1,0:T(8,128)} %pool_ref.1) | copy-start | bytes 12582916
  9.7 16.0 %copy-start.16 = (f32[2,256]{1,0:T(2,128)S(1)}, f32[2,256]{1,0:T(2,128)}, u32[]{:S(2)}) copy-start(f32[2,256]{1,0:T(2,128)} %param.25) | copy-start | bytes 6148
  9.7 16.1 %copy-start.15 = (bf16[1,3,2,256]{3,2,1,0:T(2,128)(2,1)S(1)}, bf16[1,3,2,256]{3,2,1,0:T(2,128)(2,1)}, u32[]{:S(2)}) copy-start(bf16[1,3,2,256]{3,2,1,0:T(2,128)(2,1)} %param.21) | copy-start | bytes 9220
  9.7 16.1 %copy-start.17 = (f32[32]{0:T(128)S(1)}, f32[32]{0:T(128)}, u32[]{:S(2)}) copy-start(f32[32]{0:T(128)} %param.27) | copy-start | bytes 388
  9.7 16.1 %copy-start.18 = (f32[32]{0:T(128)S(1)}, f32[32]{0:T(128)}, u32[]{:S(2)}) copy-start(f32[32]{0:T(128)} %param.26) | copy-start | bytes 388
  9.7 16.2 %copy-start.13 = (f32[4,2,256]{2,1,0:T(2,128)S(1)}, f32[4,2,256]{2,1,0:T(2,128)}, u32[]{:S(2)}) copy-start(f32[4,2,256]{2,1,0:T(2,128)} %param.24) | copy-start | bytes 24580
  9.7 16.2 %copy-start.14 = (f32[2048]{0:T(1024)S(1)}, f32[2048]{0:T(1024)}, u32[]{:S(2)}) copy-start(f32[2048]{0:T(1024)} %param.23) | copy-start | bytes 24580
  9.7 16.2 %copy-start.10 = (bf16[1,1024,32]{1,2,0:T(8,128)(2,1)S(1)}, bf16[1,1024,32]{1,2,0:T(8,128)(2,1)}, u32[]{:S(2)}) copy-start(bf16[1,1024,32]{1,2,0:T(8,128)(2,1)} %param.19) | copy-start | bytes 196612
  13.5 14.2 %copy-start.11 = (f32[4,2048]{1,0:T(4,128)S(1)}, f32[4,2048]{1,0:T(4,128)}, u32[]{:S(2)}) copy-start(f32[4,2048]{1,0:T(4,128)} %param.22) | copy-start | bytes 98308
  13.5 14.3 %copy-start.12 = (bf16[1,3,2048]{2,1,0:T(4,128)(2,1)S(1)}, bf16[1,3,2048]{2,1,0:T(4,128)(2,1)}, u32[]{:S(2)}) copy-start(bf16[1,3,2048]{2,1,0:T(4,128)(2,1)} %param.20) | copy-start | bytes 36868
  13.5 42.6 %all-to-all-start = ((bf16[64,128,128]{2,1,0:T(8,128)(2,1)}), bf16[64,128,128]{2,1,0:T(8,128)(2,1)S(1)}, u32[]{:S(2)}, u32[]{:S(2)}) async-start(bf16[64,128,128]{2,1,0:T(8,128)(2,1)} %bitcast.12), calls=%async_computation | async-start | bytes 4194304 | tf_op jit(solution)/shard_map/all_to_all | solution.py:366
  27.8 2.2 %copy-start.8 = (bf16[1,1024,2048]{2,1,0:T(8,128)(2,1)S(1)}, bf16[1,1024,2048]{2,1,0:T(8,128)(2,1)}, u32[]{:S(2)}) copy-start(bf16[1,1024,2048]{2,1,0:T(8,128)(2,1)} %param.16) | copy-start | bytes 12582916
  30.0 2.2 %copy-start.9 = (bf16[1,1024,2048]{2,1,0:T(8,128)(2,1)S(1)}, bf16[1,1024,2048]{2,1,0:T(8,128)(2,1)}, u32[]{:S(2)}) copy-start(bf16[1,1024,2048]{2,1,0:T(8,128)(2,1)} %param.17) | copy-start | bytes 12582916
  32.2 43.1 %copy-start.7 = (f32[2048]{0:T(1024)S(1)}, f32[2048]{0:T(1024)}, u32[]{:S(2)}) copy-start(f32[2048]{0:T(1024)} %param.28) | copy-start | bytes 24580
  48.4 2.0 %copy-start.1 = (bf16[1024,2048]{1,0:T(8,128)(2,1)}, bf16[1024,2048]{1,0:T(8,128)(2,1)S(1)}, u32[]{:S(2)}) copy-start(bf16[1024,2048]{1,0:T(8,128)(2,1)S(1)} %get-tuple-element.8.a_ref) | copy-start | bytes 12582916
  50.5 1.9 %copy-start.3 = (bf16[1024,2048]{1,0:T(8,128)(2,1)}, bf16[1024,2048]{1,0:T(8,128)(2,1)S(1)}, u32[]{:S(2)}) copy-start(bf16[1024,2048]{1,0:T(8,128)(2,1)S(1)} %get-tuple-element.9.b_ref) | copy-start | bytes 12582916
  52.4 0.8 copy-start.5
  53.2 17.0 %collective-permute-start.2 = (bf16[144,2048]{1,0:T(8,128)(2,1)}, bf16[144,2048]{1,0:T(8,128)(2,1)S(1)}, u32[]{:S(2)}, u32[]{:S(2)}) collective-permute-start(bf16[144,2048]{1,0:T(8,128)(2,1)} %get-tuple-element.11.mine_ref), channel_id=1, source_target_pairs={{0,64},{64,0},{1,65},{65,1},{2,66},{66,2},{3,67},{67,3},{4,68},{68... | collective-permute-start | bytes 1769480 | tf_op jit(solution)/shard_map/ppermute | solution.py:399
  56.7 18.6 %collective-permute-start.1 = (bf16[128,1024]{1,0:T(8,128)(2,1)S(1)}, bf16[128,1024]{1,0:T(8,128)(2,1)S(1)}, u32[]{:S(2)}, u32[]{:S(2)}) collective-permute-start(bf16[128,1024]{1,0:T(8,128)(2,1)S(1)} %select_states.1.own_ref), channel_id=1, source_target_pairs={{0,64},{64,0},{1,65},{65,1},{2,66},{66,2},{3,67},{67,3},{4,68},{68... | collective-permute-start | bytes 786440 | tf_op jit(solution)/shard_map/ppermute | solution.py:402
  75.3 2.2 %copy-start.2 = (bf16[1024,2048]{1,0:T(8,128)(2,1)S(1)}, bf16[1024,2048]{1,0:T(8,128)(2,1)}, u32[]{:S(2)}) copy-start(bf16[1024,2048]{1,0:T(8,128)(2,1)} %copy-done.1) | copy-start | bytes 12582916
  77.5 2.2 %copy-start.4 = (bf16[1024,2048]{1,0:T(8,128)(2,1)S(1)}, bf16[1024,2048]{1,0:T(8,128)(2,1)}, u32[]{:S(2)}) copy-start(bf16[1024,2048]{1,0:T(8,128)(2,1)} %copy-done.3) | copy-start | bytes 12582916
  79.7 1.0 %copy-start.6 = (bf16[1024,256]{1,0:T(8,128)(2,1)S(1)}, bf16[1024,256]{1,0:T(8,128)(2,1)}, u32[]{:S(2)}) copy-start(bf16[1024,256]{1,0:T(8,128)(2,1)} %copy-done.5) | copy-start | bytes 1572868

commit v2 on v1

v2 whole, which is shorter than its diff:
```python
import functools

import jax
import jax.numpy as jnp
from jax import lax
from jax.experimental import pallas as pl
from jax.experimental.pallas import tpu as pltpu
from jax.sharding import PartitionSpec as P

BLK = 128
EPS = 1e-05
JOIN_ROWS = 512
LOCAL_ROWS = 256
MIB = 1 << 20
VMEM_LIMIT = 56 * MIB
F32 = jnp.float32
BF16 = jnp.bfloat16
SMEM = pltpu.SMEM
VMEM = pltpu.VMEM


def dot(a, b):
    return jnp.dot(a, b, preferred_element_type=F32)


def silu(v):
    half = 0.5 * v
    return half * jnp.tanh(half) + half


def split_two(v):
    high = v.astype(BF16)
    return high, (v - high.astype(F32)).astype(BF16)


def split_three(v):
    high = v.astype(BF16)
    rest = v - high.astype(F32)
    mid = rest.astype(BF16)
    return high, mid, (rest - mid.astype(F32)).astype(BF16)


def iota(shape, dim):
    return lax.broadcasted_iota(jnp.int32, shape, dim)


def over(v, power_of_two):
    return lax.shift_right_logical(v, jnp.int32(power_of_two.bit_length() - 1))


def edge_kernel(x_ref, bc_ref, edge_ref):
    width = x_ref.shape[1]
    edge_ref[:, :width] = x_ref[...]
    rows = bc_ref[...].astype(F32)
    for group in range(bc_ref.shape[1]):
        at = width + group * bc_ref.shape[2]
        edge_ref[:, at : at + bc_ref.shape[2]] = rows[:, group, :].astype(BF16)


def edge_of(x, bc):
    last = x.shape[0] // 16 - 1
    edge = (16, x.shape[1] + bc.shape[1] * bc.shape[2])
    return pl.pallas_call(
        edge_kernel,
        out_shape=jax.ShapeDtypeStruct(edge, BF16),
        grid=(1,),
        in_specs=[
            pl.BlockSpec((16, x.shape[1]), lambda i: (last, 0)),
            pl.BlockSpec((16,) + bc.shape[1:], lambda i: (last, 0, 0)),
        ],
        out_specs=pl.BlockSpec(edge, lambda i: (0, 0)),
        compiler_params=pltpu.CompilerParams(vmem_limit_bytes=VMEM_LIMIT),
        cost_estimate=pl.CostEstimate(flops=0, bytes_accessed=MIB // 4, transcendentals=0),
        name="edge_rows",
    )(x, bc)


def pack_kernel(
    slots_ref, pool_hbm, edge_hbm, out_ref,
    pool, keys, keys_smem, pool_sems, keys_sem,
):
    step = pl.program_id(0)
    section_count = lax.axis_size("section")
    mp_count = lax.axis_size("mp")
    peer_count = lax.axis_size("cache") * mp_count
    slots_dev = pool.shape[0]
    count = out_ref.shape[0]
    heads = slots_ref.shape[1]
    share = heads // mp_count
    quarter = share // section_count
    held = slots_dev // peer_count
    section = lax.axis_index("section")

    @pl.when(step == 0)
    def _():
        part = slots_dev // pool_sems.shape[0]
        copies = []
        for k in range(pool_sems.shape[0]):
            rows = pl.ds(k * part, part)
            copies.append(pltpu.make_async_copy(pool_hbm.at[rows], pool.at[rows], pool_sems.at[k]))
        for copy in copies:
            copy.start()
        me = lax.axis_index("cache") * mp_count + lax.axis_index("mp")
        slots = slots_ref[...]
        lane = iota(slots.shape, 1)
        mine = lax.rem(lax.div(slots, slots_dev), peer_count) == me
        key = lane * slots_dev + lax.rem(slots, slots_dev)
        first = jnp.where(mine, key, heads * slots_dev)
        last = jnp.where(mine, key, 0)
        shift = 1
        while shift < quarter:
            first = jnp.minimum(first, pltpu.roll(first, heads - shift, 1))
            last = jnp.maximum(last, pltpu.roll(last, heads - shift, 1))
            shift *= 2
        keys[0] = lax.rem(first, slots_dev)
        keys[1] = lax.rem(last, slots_dev)
        listing = pltpu.make_async_copy(keys, keys_smem, keys_sem)
        listing.start()
        listing.wait()
        for copy in copies:
            copy.wait()

    base = step * (count // held)

    def one(i, carry):
        dest = base + i
        row = lax.div(dest, mp_count)
        col = lax.rem(dest, mp_count) * share + section * quarter
        for k in range(held):
            out_ref[held * i + k] = pool[keys_smem[k, row, col]].astype(BF16)
        return carry

    lax.fori_loop(0, count // held, one, 0, unroll=8)


def pack(slots, pool, edge):
    steps = 4
    count = pool.shape[0] // steps
    return pl.pallas_call(
        pack_kernel,
        out_shape=jax.ShapeDtypeStruct(pool.shape, BF16),
        grid=(steps,),
        in_specs=[
            pl.BlockSpec(slots.shape, lambda i: (0, 0)),
            pl.BlockSpec(memory_space=pl.ANY),
            pl.BlockSpec(memory_space=pl.ANY),
        ],
        out_specs=pl.BlockSpec((count,) + pool.shape[1:], lambda i: (i, 0, 0)),
        scratch_shapes=[
            VMEM(pool.shape, F32),
            VMEM((2,) + slots.shape, jnp.int32),
            SMEM((2,) + slots.shape, jnp.int32),
            pltpu.SemaphoreType.DMA((4,)),
            pltpu.SemaphoreType.DMA,
        ],
        compiler_params=pltpu.CompilerParams(vmem_limit_bytes=VMEM_LIMIT),
        cost_estimate=pl.CostEstimate(flops=0, bytes_accessed=6 * MIB, transcendentals=0),
        name="pack_states",
    )(slots, pool, edge)


def select_kernel(slots_ref, incoming_ref, out_ref, *, slots_dev, held):
    section_count = lax.axis_size("section")
    mp_count = lax.axis_size("mp")
    peer_count = lax.axis_size("cache") * mp_count
    share = slots_ref.shape[1] // mp_count
    quarter = share // section_count
    row = lax.axis_index("cache")
    at = lax.axis_index("mp") * share + lax.axis_index("section") * quarter
    owners, index = [], []
    for h in range(quarter):
        owner = lax.rem(lax.div(slots_ref[row, at + h], slots_dev), peer_count)
        again = jnp.int32(0)
        for earlier in owners:
            again = jnp.where(earlier == owner, 1, again)
        owners.append(owner)
        index.append(owner * held + again)
    for pair in range(quarter // 2):
        two = jnp.concatenate(
            [incoming_ref[index[2 * pair + k]].astype(F32) for k in range(2)], 0
        )
        out_ref[:, pair * BLK : (pair + 1) * BLK] = two.T.astype(BF16)


def select(slots, incoming, quarter, held):
    count, head_dim, state_size = incoming.shape
    return pl.pallas_call(
        functools.partial(select_kernel, slots_dev=count, held=held),
        out_shape=jax.ShapeDtypeStruct((state_size, quarter * head_dim), BF16),
        in_specs=[pl.BlockSpec(memory_space=SMEM), pl.BlockSpec(memory_space=VMEM)],
        out_specs=pl.BlockSpec(memory_space=VMEM),
        compiler_params=pltpu.CompilerParams(vmem_limit_bytes=VMEM_LIMIT),
        cost_estimate=pl.CostEstimate(flops=0, bytes_accessed=3 * MIB, transcendentals=0),
        name="select_states",
    )(slots, incoming)


def local_kernel(
    len_ref, x_ref, z_ref, bc_ref, dt_ref, bias_ref, rate_ref, got_ref,
    tail_x_ref, tail_bc_ref, tap_x_ref, off_x_ref, tap_bc_ref, off_bc_ref, *rest,
    group, blocks, head_dim,
):
    a_ref, b_ref, c_ref, t_ref, spread, factors, behind, state, decay = rest[-9:]
    step = pl.program_id(0)
    width = x_ref.shape[1]
    heads = width // head_dim
    state_size = bc_ref.shape[1] // 2
    per_step = x_ref.shape[0] // BLK
    chunk = 256
    here = slice(group * heads, (group + 1) * heads)

    @pl.when(step == 0)
    def _():
        section = lax.axis_index("section")
        got_x = got_ref[:, group * width : (group + 1) * width].astype(F32)[8:]
        at = lax.axis_size("section") * width + group * 2 * state_size
        got_bc = got_ref[:, at : at + 2 * state_size].astype(F32)[8:]
        behind[:, :width] = got_x
        behind[:, width:] = got_bc

        @pl.when(section == 0)
        def _():
            behind[5:8, :width] = tail_x_ref[:, group * width : (group + 1) * width].astype(F32)
            behind[5:8, width:] = tail_bc_ref[:, group, :].astype(F32)

        state[...] = jnp.zeros_like(state)
        decay[...] = jnp.ones_like(decay)
        for at in range(0, width, BLK):
            shape = (spread.shape[0], BLK)
            head = over(iota(shape, 1) + at, head_dim)
            spread[:, at : at + BLK] = jnp.where(
                (iota(shape, 0) & (heads - 1)) == head, 1.0, 0.0
            ).astype(BF16)
        raw = dt_ref[here, :].astype(F32)
        stacked = lambda v: jnp.concatenate([v] * blocks, 0)
        value = jnp.concatenate([raw[:, k * BLK : (k + 1) * BLK] for k in range(blocks)], 0)
        flat = jnp.concatenate(
            [bias_ref[...], rate_ref[...], jnp.zeros((1, BLK - 2 * bias_ref.shape[1]), F32)], 1
        )
        turned = jnp.broadcast_to(flat, (BLK, BLK)).T
        value = value + stacked(turned[here])
        soft = jnp.maximum(value, 0.0) + jnp.log1p(jnp.exp(-jnp.abs(value)))
        shape = value.shape
        position = (
            section * (blocks * BLK) + over(iota(shape, 0), heads) * BLK + iota(shape, 1)
        )
        steps = jnp.where(position < len_ref[0], soft, 0.0)
        log_decay = -steps * stacked(
            turned[bias_ref.shape[1] + group * heads : bias_ref.shape[1] + (group + 1) * heads]
        )
        upper = jnp.where(iota((BLK, BLK), 0) <= iota((BLK, BLK), 1), 1.0, 0.0).astype(BF16)
        cum_log = sum(dot(part, upper) for part in split_three(log_decay))
        owner = over(iota((BLK, BLK), 1), heads)
        for row, full in enumerate((jnp.exp(cum_log), steps * jnp.exp(-cum_log))):
            for part, values in enumerate(split_two(full.T)):
                values = values.astype(F32)
                for block in range(blocks):
                    factors[
                        block, row * BLK : (row + 1) * BLK, part * BLK : (part + 1) * BLK
                    ] = jnp.where(owner == block, values, 0.0).astype(BF16)

    def conv(source, at, size, base, taps, offset):
        now = source[rows, at : at + size].astype(F32)
        cols = slice(base + at, base + at + size)
        joined = jnp.concatenate([behind[:, cols], now], 0)
        total = offset + taps[3:4] * now
        for k in range(3):
            total = total + taps[k : k + 1] * joined[5 + k : 5 + k + BLK]
        behind[:, cols] = now[BLK - 8 :]
        return silu(total)

    causal = iota((BLK, BLK), 0) >= iota((BLK, BLK), 1)
    for sub in range(per_step):
        rows = slice(sub * BLK, (sub + 1) * BLK)
        mixed = conv(
            bc_ref, 0, 2 * state_size, width,
            tap_bc_ref[:, group, :], off_bc_ref[group : group + 1, :],
        )
        c_block = mixed[:, state_size:].astype(BF16)
        b_turned = mixed[:, :state_size].T.astype(BF16)
        c_ref[rows, :] = c_block
        scores = jnp.where(causal, dot(c_block, b_turned), 0.0).astype(BF16)
        left = jnp.concatenate([scores, c_block], 1)
        factor = factors[step * per_step + sub]
        for at in range(0, width, chunk):
            cols = slice(at, at + chunk)
            x_conv = conv(x_ref, at, chunk, 0, tap_x_ref[:, cols], off_x_ref[:, cols])
            scale = dot(factor, spread[:, cols])
            risen = scale[:BLK]
            inner = (x_conv * scale[BLK:]).astype(BF16)
            before = state[:, cols]
            y_local = risen * dot(left, jnp.concatenate([inner, before.astype(BF16)], 0))
            last = risen[BLK - 1 :]
            state[:, cols] = last * (before + dot(b_turned, inner))
            gate = silu(z_ref[rows, cols].astype(F32))
            passed = decay[0:1, cols]
            a_ref[rows, cols] = (y_local * gate).astype(BF16)
            b_ref[rows, cols] = (risen * passed * gate).astype(BF16)
            decay[0:1, cols] = passed * last

    @pl.when(step == pl.num_programs(0) - 1)
    def _():
        t_ref[:BLK] = state[...].astype(BF16)
        row = iota((16, width), 0)
        parts = jnp.zeros((16, width), F32)
        for k, part in enumerate(split_three(decay[0:1, :])):
            parts = jnp.where(row == k, part.astype(F32), parts)
        t_ref[BLK:] = parts.astype(BF16)


def local_part(group, groups, length, x, z, bc, dt, params, received, into):
    bias, rate, tail_x, tail_bc, tap_x, off_x, tap_bc, off_bc = params
    seg_len, channels = x.shape
    blocks = seg_len // BLK
    width = channels // groups
    head_dim = channels // dt.shape[0]
    pair = bc.shape[1] // groups
    body = functools.partial(local_kernel, group=group, blocks=blocks, head_dim=head_dim)
    by_block = lambda size: pl.BlockSpec((LOCAL_ROWS, size), lambda i: (i, group))
    whole = lambda shape: pl.BlockSpec(shape, lambda i: (0,) * len(shape))
    column = lambda size: pl.BlockSpec((size, width), lambda i: (0, group))
    shapes = (
        jax.ShapeDtypeStruct((seg_len, channels), BF16),
        jax.ShapeDtypeStruct((seg_len, channels), BF16),
        jax.ShapeDtypeStruct((seg_len, groups * pair // 2), BF16),
        jax.ShapeDtypeStruct((BLK + 16, width), BF16),
    )
    operands = (
        length, x, z, bc, dt, bias, rate, received, tail_x, tail_bc, tap_x, off_x, tap_bc, off_bc,
    )
    return pl.pallas_call(
        body,
        out_shape=shapes,
        grid=(seg_len // LOCAL_ROWS,),
        in_specs=[
            pl.BlockSpec(memory_space=SMEM),
            by_block(width), by_block(width), by_block(pair),
            whole(dt.shape), whole(bias.shape), whole(rate.shape), whole(received.shape),
            whole(tail_x.shape), whole(tail_bc.shape),
            column(tap_x.shape[0]), column(1), whole(tap_bc.shape), whole(off_bc.shape),
        ] + [pl.BlockSpec(memory_space=pl.ANY)] * len(into),
        out_specs=(
            by_block(width), by_block(width), by_block(pair // 2), whole((BLK + 16, width)),
        ),
        scratch_shapes=[
            VMEM((2 * BLK, width), BF16),
            VMEM((blocks, 2 * BLK, 2 * BLK), BF16),
            VMEM((8, width + pair), F32),
            VMEM((BLK, width), F32),
            VMEM((8, width), F32),
        ],
        input_output_aliases={len(operands) + k: k for k in range(len(into))},
        compiler_params=pltpu.CompilerParams(vmem_limit_bytes=VMEM_LIMIT),
        cost_estimate=pl.CostEstimate(
            flops=2 * seg_len * width * 1024, bytes_accessed=10 * MIB,
            transcendentals=2 * seg_len * width,
        ),
        name="local_blocks",
    )(*operands, *into)


def decay_of(ref, cols):
    rows = ref[BLK : BLK + 16, cols].astype(F32)
    return rows[0:1] + rows[1:2] + rows[2:3]


def moved(ref, cols, cached):
    return decay_of(ref, cols) * cached + ref[:BLK, cols].astype(F32)


def join_kernel(
    group_ref, len_ref, a_ref, b_ref, c_ref, cached_ref, before_ref, gain_ref, *rest, ending
):
    if ending:
        own_ref, mine0_ref, theirs0_ref, mine1_ref, theirs1_ref, _ = rest[:6]
        out_ref, final_ref, start, gated = rest[6:]
    else:
        out_ref, start, gated = rest
    step = pl.program_id(0)
    section = lax.axis_index("section")
    width = a_ref.shape[1]
    chunk = 256

    @pl.when(step == 0)
    def _():
        @pl.when(section == 0)
        def _():
            start[...] = cached_ref[...]

        @pl.when(section == 1)
        def _():
            for at in range(0, width, chunk):
                cols = slice(at, at + chunk)
                start[:, cols] = moved(before_ref, cols, cached_ref[:, cols].astype(F32)).astype(BF16)

    if ending:
        last = pl.num_programs(0) - 1
        orders = ((mine0_ref, theirs0_ref), (theirs1_ref, mine1_ref))
        for place, (early_ref, late_ref) in enumerate(orders):

            @pl.when((step == last) & (section == place))
            def _(early_ref=early_ref, late_ref=late_ref):
                for at in range(0, width, BLK):
                    cols = slice(at, at + BLK)
                    middle = moved(early_ref, cols, own_ref[:, cols].astype(F32))
                    final_ref[cols, :] = moved(late_ref, cols, middle).T

    size = a_ref.shape[0]
    position = (section * pl.num_programs(0) + step) * size + iota((size, 1), 0)
    live = (position < len_ref[0]).astype(F32)
    c_block = c_ref[...]
    squares = jnp.zeros((size, BLK), F32)
    for at in range(0, width, chunk):
        cols = slice(at, at + chunk)
        inter = dot(c_block, start[:, cols])
        value = a_ref[:, cols].astype(F32) + b_ref[:, cols].astype(F32) * inter
        gated[:, cols] = value
        square = value * value
        for k in range(chunk // BLK):
            squares = squares + square[:, k * BLK : (k + 1) * BLK]
    mean = jnp.sum(squares, 1, keepdims=True) * (1.0 / width)
    scale = lax.rsqrt(mean + EPS) * live
    for at in range(0, width, chunk):
        cols = slice(at, at + chunk)
        out_ref[:, cols] = (gated[:, cols] * scale * gain_ref[:, cols]).astype(BF16)


def join_part(group, groups, length, a, b, c, cached, before, gain, ending=()):
    seg_len, channels = a.shape
    width = channels // groups
    by_block = lambda size: pl.BlockSpec((JOIN_ROWS, size), lambda i, at: (i, at[0]))
    whole = lambda shape: pl.BlockSpec(shape, lambda i, at: (0,) * len(shape))
    out_shape = [jax.ShapeDtypeStruct((seg_len, channels), BF16)]
    out_specs = [by_block(width)]
    extra = []
    aliases = {}
    if ending:
        final_shape = (cached.shape[1], cached.shape[0])
        out_shape.append(jax.ShapeDtypeStruct(final_shape, F32))
        out_specs.append(whole(final_shape))
        extra = [whole(v.shape) for v in ending[:-1]] + [pl.BlockSpec(memory_space=pl.ANY)]
        aliases = {8 + len(ending) - 1: 0}
    return pl.pallas_call(
        functools.partial(join_kernel, ending=bool(ending)),
        out_shape=out_shape,
        grid_spec=pltpu.PrefetchScalarGridSpec(
            num_scalar_prefetch=1,
            grid=(seg_len // JOIN_ROWS,),
            in_specs=[
                pl.BlockSpec(memory_space=SMEM),
                by_block(width), by_block(width), by_block(c.shape[1] // groups),
                whole(cached.shape), whole(before.shape),
                pl.BlockSpec((1, width), lambda i, at: (0, at[0])),
            ] + extra,
            out_specs=out_specs,
            scratch_shapes=[VMEM((BLK, width), BF16), VMEM((JOIN_ROWS, width), F32)],
        ),
        input_output_aliases=aliases,
        compiler_params=pltpu.CompilerParams(vmem_limit_bytes=VMEM_LIMIT),
        cost_estimate=pl.CostEstimate(
            flops=2 * seg_len * width * BLK, bytes_accessed=7 * MIB, transcendentals=0
        ),
        name="join_blocks",
    )(group, length, a, b, c, cached, before, gain, *ending)


def body(
    x_in,
    z_in,
    bc_in,
    dt_in,
    tail_x,
    tail_bc,
    conv_w_x,
    conv_b_x,
    conv_w_bc,
    conv_b_bc,
    dt_bias,
    decay_rate,
    norm_gain,
    state_pool,
    block_slots,
    new_len,
):
    section = lax.axis_index("section").astype(jnp.int32)
    section_count = lax.axis_size("section")
    peer_count = lax.axis_size("cache") * lax.axis_size("mp")
    _, seg_len, channels = x_in.shape
    groups = bc_in.shape[2]
    state_size = bc_in.shape[3] // 2
    head_count = dt_in.shape[2]
    head_dim = channels // head_count
    quarter = head_count // section_count
    slots_dev = state_pool.shape[0]
    held = slots_dev // peer_count
    forth, swap = [(0, 1)], [(0, 1), (1, 0)]

    edge = edge_of(x_in[0], bc_in[0])
    received = lax.ppermute(edge, "section", forth)
    outgoing = pack(block_slots, state_pool, edge)
    outgoing, received = lax.optimization_barrier((outgoing, received))
    incoming = lax.all_to_all(
        outgoing.reshape(peer_count, held * head_dim, state_size),
        ("cache", "mp"), split_axis=0, concat_axis=0, tiled=True,
    )

    bc2 = bc_in[0].reshape(seg_len, groups * 2 * state_size)
    params = (
        dt_bias[None], decay_rate[None], tail_x[0], tail_bc[0],
        conv_w_x, conv_b_x[None], conv_w_bc, conv_b_bc,
    )
    shared = (new_len, x_in[0], z_in[0], bc2, dt_in[0].T, params, received)
    a, b, c, mine1 = local_part(1, groups, *shared, ())
    theirs1 = lax.ppermute(mine1, "section", forth)
    a, b, c, mine0 = local_part(0, groups, *shared, (a, b, c))
    theirs0 = lax.ppermute(mine0, "section", swap)

    own = select(
        block_slots, incoming.reshape(peer_count * held, head_dim, state_size), quarter, held
    )
    other = lax.ppermute(own, "section", swap)
    gain = norm_gain[None]
    (gated,) = join_part(section[None], groups, new_len, a, b, c, own, theirs1, gain)
    gated, final = join_part(
        1 - section[None], groups, new_len, a, b, c, other, theirs0, gain,
        (own, mine0, theirs0, mine1, theirs1, gated),
    )
    return (
        gated[None],
        final.reshape(1, 1, 1, quarter, head_dim, state_size),
    )


def solution(mesh):
    in_specs = (
        P("cache", "section", "mp"),
        P("cache", "section", "mp"),
        P("cache", "section", "mp", None),
        P("cache", "section", "mp"),
        P("cache", None, "mp"),
        P("cache", None, "mp", None),
        P(None, "mp"),
        P("mp"),
        P(None, "mp", None),
        P("mp", None),
        P("mp"),
        P("mp"),
        P("mp"),
        P(("section", "cache", "mp"), None, None),
        P(),
        P("cache"),
    )
    out_specs = (P("cache", "section", "mp"), P("cache", "mp", "section", None, None, None))
    return jax.shard_map(body, mesh=mesh, in_specs=in_specs, out_specs=out_specs, check_vma=False)
```

time: 90.2 us -> 71 us (0.79); the launches traced: 88.5 us -> 70.5 us
  local copies, waits for them, and re-layouts: 21.3 us -> 3.97 us
  waiting for transfers between devices: 18.5 us -> 5.8 us
  Pallas kernels: 28.4 us -> 40.3 us
  starting transfers between devices: 15.6 us -> 19.1 us
  other arithmetic: 3.08 us -> 0 us
    unnamed x44 -> x13, local copies, waits for them, and re-layouts: 18.2 us -> 3.97 us
    ppermute x2 -> x3, waiting for transfers between devices: 13.3 us -> 0.65 us  [the longest x1 0.39 us: body(): theirs0 = lax.ppermute(mine0, 'section', swap)]
    pallas_call x4 -> x7, Pallas kernels: 28.4 us -> 40.3 us  [the longest x2 21 us: local_part(): pl.pallas_call(body, out_shape=shapes, grid=(seg_len // LOCAL_ROWS,), in_...]
    reduce_min x1 -> x0, other arithmetic: 2.37 us -> none  [body(): first = jnp.min(jnp.where(mine, key, quarter * slots_dev), 1) % slots_dev]
    ppermute x1, starting transfers between devices: 0.09 us -> 2.17 us  [body(): other = lax.ppermute(own, 'section', swap)]
    slice x2 -> x0, local copies, waits for them, and re-layouts: 1.58 us -> none  [the longest x1 0.85 us: body(): x2[seg_len - 16:]]
    ppermute x2 -> x3, starting transfers between devices: 3.93 us -> 5.44 us  [the longest x1 2.74 us: body(): theirs0 = lax.ppermute(mine0, 'section', swap)]
    reshape x3 -> x0, local copies, waits for them, and re-layouts: 1.07 us -> none  [the longest x1 0.83 us: body(): listed = block_slots.reshape(cache_count, mp_count, section_count, quarter)]
  transfers between devices with their start and end apart: 4 -> 5, of which waited for: 2 -> 3; matrix products, arithmetic and copies ran while one was open for 7% -> 2% of each run, Pallas kernels for 23% -> 47%
where the time goes in v2:
time: 71 us; the launch traced here: 70.5 us
  Pallas kernels  40.3 us (57%)
  starting transfers between devices  19.1 us (27%)
  waiting for transfers between devices  5.8 us (8%)
  local copies, waits for them, and re-layouts  3.97 us (6%)
  between operations  1.34 us (2%)
    pallas_call x2, Pallas kernels, local_part(): pl.pallas_call(body, out_shape=shapes, grid=(seg_len // LOCAL_ROWS,), in_...  21 us
    all_to_all x1, starting transfers between devices, body(): lax.all_to_all(outgoing.reshape(peer_count, held * head_dim, state_size),...  11.5 us
    pallas_call x2, Pallas kernels, join_part(): pl.pallas_call(functools.partial(join_kernel, ending=bool(ending)), out_s...  10.3 us
    ppermute x1, waiting for transfers between devices, body(): other = lax.ppermute(own, 'section', swap)  5.14 us
    pallas_call x1, Pallas kernels, pack(): pl.pallas_call(pack_kernel, out_shape=jax.ShapeDtypeStruct(pool.shape, BF...  4.97 us
    unnamed x13, local copies, waits for them, and re-layouts  3.97 us
    ppermute x1, starting transfers between devices, body(): theirs0 = lax.ppermute(mine0, 'section', swap)  2.74 us
    pallas_call x1, Pallas kernels, select(): pl.pallas_call(functools.partial(select_kernel, slots_dev=count, held=hel...  2.57 us
  transfers between devices with their start and end apart: 5, of which 3 were waited for; matrix products, arithmetic and copies ran while one was open for 2% of the time, Pallas kernels for 47%

profile of v2, /device:TPU:6, one launch (start us, length us, event | category | flops | bytes accessed | tf_op | source)
XLA Modules:
  0.0 70.5 jit_solution(9099443459071283854)
XLA Ops:
  0.6 1.5 %edge_rows.1.edge_hbm = bf16[16,2560]{1,0:T(8,128)(2,1)} custom-call(bf16[1024,2048]{1,0:T(8,128)(2,1)} %bitcast.20, bf16[1024,2,256]{2,1,0:T(2,128)(2,1)} %bitcast.30), custom_call_target="tpu_custom_call" | custom-call | bytes 262144 | tf_op jit(solution)/shard_map/edge_rows/pallas_call | solution.py:63
  2.2 0.0 copy-start.1
  2.2 1.4 %collective-permute-start = (bf16[16,2560]{1,0:T(8,128)(2,1)}, bf16[16,2560]{1,0:T(8,128)(2,1)S(1)}, u32[]{:S(2)}, u32[]{:S(2)}) collective-permute-start(bf16[16,2560]{1,0:T(8,128)(2,1)} %edge_rows.1.edge_hbm), channel_id=1, source_target_pairs={{0,64},{1,65},{2,66},{3,67},{4,68},{5,69},{6,70},{7,71},{8,72},{9,... | collective-permute-start | bytes 245768 | tf_op jit(solution)/shard_map/ppermute | solution.py:499
  3.6 5.0 %pack_states.1 = bf16[128,64,128]{2,1,0:T(8,128)(2,1)} custom-call(s32[16,128]{1,0:T(8,128)} %slots_ref.3, f32[128,64,128]{2,1,0:T(8,128)} %pool_hbm.1, bf16[16,2560]{1,0:T(8,128)(2,1)} %edge_rows.1.edge_hbm), custom_call_target="tpu_custom_call" | custom-call | bytes 6291456 | tf_op jit(solution)/shard_map/pack_states/pallas_call | solution.py:139
  8.6 0.3 collective-permute-done.got_ref
  8.8 0.0 copy-start.4
  8.8 11.5 %all-to-all-start = ((bf16[64,128,128]{2,1,0:T(8,128)(2,1)}), bf16[64,128,128]{2,1,0:T(8,128)(2,1)S(1)}, u32[]{:S(2)}, u32[]{:S(2)}) async-start(bf16[64,128,128]{2,1,0:T(8,128)(2,1)} %bitcast.29), calls=%async_computation | async-start | bytes 4194304 | tf_op jit(solution)/shard_map/all_to_all | solution.py:502
  21.0 0.0 copy-done.1
  21.0 1.2 %copy.22 = bf16[128,8,2,256]{3,1,2,0:T(8,128)(2,1)} copy(bf16[128,8,2,256]{3,2,1,0:T(2,128)(2,1)S(1)} %bitcast.31) | data formatting | bytes 2097152
  22.2 0.0 copy-done.4
  22.2 10.5 %local_blocks.2 = (bf16[1024,2048]{1,0:T(8,128)(2,1)}, bf16[1024,2048]{1,0:T(8,128)(2,1)}, bf16[1024,256]{1,0:T(8,128)(2,1)}, bf16[144,1024]{1,0:T(8,128)(2,1)}) custom-call(s32[1]{0:T(128)S(6)} %copy.27.len_ref, bf16[1024,2048]{1,0:T(8,128)(2,1)} %bitcast.21, bf16[1024,2048]{1,0:T(8,128)(2,1)} %bitcast.24, bf16[1024,512]{1,0:T(8,128)(2,1)} %bitcast.26, ...), custom_call_target="tpu_custom_call" | custom-call | flops 2147483648 | bytes 10485760 | tf_op jit(solution)/shard_map/local_blocks/pallas_call | solution.py:331
  32.7 1.3 %collective-permute-start.3 = (bf16[144,1024]{1,0:T(8,128)(2,1)}, bf16[144,1024]{1,0:T(8,128)(2,1)S(1)}, u32[]{:S(2)}, u32[]{:S(2)}) collective-permute-start(bf16[144,1024]{1,0:T(8,128)(2,1)} %get-tuple-element.23.rest_3_), channel_id=1, source_target_pairs={{0,64},{1,65},{2,66},{3,67},{4,68},{5,69},{6,70},{7,71},{8,72},{9,... | collective-permute-start | bytes 884744 | tf_op jit(solution)/shard_map/ppermute | solution.py:514
  34.0 10.5 %local_blocks.3 = (bf16[1024,2048]{1,0:T(8,128)(2,1)}, bf16[1024,2048]{1,0:T(8,128)(2,1)}, bf16[1024,256]{1,0:T(8,128)(2,1)}, bf16[144,1024]{1,0:T(8,128)(2,1)}) custom-call(s32[1]{0:T(128)S(6)} %copy.27.len_ref, bf16[1024,2048]{1,0:T(8,128)(2,1)} %bitcast.22, ...), custom_call_target="tpu_custom_call", output_to_operand_aliasing={{0}: (14, {}), {1}: (15, {}), {2}: (16, {})} | custom-call | flops 2147483648 | bytes 10485760 | tf_op jit(solution)/shard_map/local_blocks/pallas_call | solution.py:331
  44.5 2.7 %collective-permute-start.2 = (bf16[144,1024]{1,0:T(8,128)(2,1)}, bf16[144,1024]{1,0:T(8,128)(2,1)S(1)}, u32[]{:S(2)}, u32[]{:S(2)}) collective-permute-start(bf16[144,1024]{1,0:T(8,128)(2,1)} %get-tuple-element.22.rest_1_), channel_id=1, source_target_pairs={{0,64},{64,0},{1,65},{65,1},{2,66},{66,2},{3,67},{67,3},{4,68},{68... | collective-permute-start | bytes 884744 | tf_op jit(solution)/shard_map/ppermute | solution.py:516
  47.2 0.0 all-to-all-done
  47.2 0.0 copy-start
  47.2 1.3 %copy-done = bf16[64,128,128]{2,1,0:T(8,128)(2,1)} copy-done((bf16[64,128,128]{2,1,0:T(8,128)(2,1)}, bf16[64,128,128]{2,1,0:T(8,128)(2,1)S(1)}, u32[]{:S(2)}) %copy-start) | copy-done | bytes 2097176
  48.5 2.6 %select_states.1.cached_ref.rest_0_ = bf16[128,1024]{1,0:T(8,128)(2,1)} custom-call(s32[16,128]{1,0:T(8,128)} %slots_ref.3, bf16[128,64,128]{2,1,0:T(8,128)(2,1)} %bitcast.28), custom_call_target="tpu_custom_call" | custom-call | bytes 3145728 | tf_op jit(solution)/shard_map/select_states/pallas_call | solution.py:187
  51.1 2.2 %collective-permute-start.1 = (bf16[128,1024]{1,0:T(8,128)(2,1)}, bf16[128,1024]{1,0:T(8,128)(2,1)S(1)}, u32[]{:S(2)}, u32[]{:S(2)}) collective-permute-start(bf16[128,1024]{1,0:T(8,128)(2,1)} %select_states.1.cached_ref.rest_0_), channel_id=1, source_target_pairs={{0,64},{64,0},{1,65},{65,1},{2,66},{66,2},{3,67},{67,3},{4,68},{68... | collective-permute-start | bytes 786440 | tf_op jit(solution)/shard_map/ppermute | solution.py:521
  53.3 0.0 collective-permute-done.3.before_ref.rest_4_
  53.3 0.0 copy-start.2
  53.3 0.7 %copy-done.2 = bf16[144,1024]{1,0:T(8,128)(2,1)} copy-done((bf16[144,1024]{1,0:T(8,128)(2,1)}, bf16[144,1024]{1,0:T(8,128)(2,1)S(1)}, u32[]{:S(2)}) %copy-start.2) | copy-done | bytes 294936
  54.0 4.8 %join_blocks.2.rest_5_ = bf16[1024,2048]{1,0:T(8,128)(2,1)} custom-call(s32[1]{0:T(128)} %bitcast.group_ref, s32[1]{0:T(128)S(6)} %copy.27.len_ref, bf16[1024,2048]{1,0:T(8,128)(2,1)} %get-tuple-element.18.a_ref, bf16[1024,2048]{1,0:T(8,128)(2,1)} %get-tuple-element.19.b_ref, bf16[1024,256]{1,0:T(8,128)(2,1)} %get-tuple-element.20.c_ref, ...), custom_call_target="tpu_custom_call" | custom-call | flops 268435456 | bytes 7340032 | tf_op jit(solution)/shard_map/join_blocks/pallas_call | solution.py:443
  58.8 0.4 collective-permute-done.2.before_ref.rest_2_
  59.1 0.0 copy-start.3
  59.1 5.1 %collective-permute-done.1.cached_ref = bf16[128,1024]{1,0:T(8,128)(2,1)S(1)} collective-permute-done((bf16[128,1024]{1,0:T(8,128)(2,1)}, bf16[128,1024]{1,0:T(8,128)(2,1)S(1)}, u32[]{:S(2)}, u32[]{:S(2)}) %collective-permute-start.1) | collective-permute-done | bytes 262176 | tf_op jit(solution)/shard_map/ppermute | solution.py:521
  64.3 0.0 copy-done.3
  64.3 0.0 copy-start.5
  64.3 0.7 copy-done.5
  65.0 5.5 %join_blocks.3 = (bf16[1024,2048]{1,0:T(8,128)(2,1)}, f32[1024,128]{1,0:T(8,128)}) custom-call(s32[1]{0:T(128)S(6)} %sub.3.group_ref, s32[1]{0:T(128)S(6)} %copy.27.len_ref, bf16[1024,2048]{1,0:T(8,128)(2,1)} %get-tuple-element.18.a_ref, bf16[1024,2048]{1,0:T(8,128)(2,1)} %get-tuple-element.19.b_ref, ...), custom_call_target="tpu_custom_call", output_to_operand_aliasing={{0}: (13, {})} | custom-call | flops 268435456 | bytes 7340032 | tf_op jit(solution)/shard_map/join_blocks/pallas_call | solution.py:443
Async XLA Ops:
  2.2 18.8 %copy-start.1 = (bf16[1,1024,2,256]{3,2,1,0:T(2,128)(2,1)S(1)}, bf16[1,1024,2,256]{3,2,1,0:T(2,128)(2,1)}, u32[]{:S(2)}) copy-start(bf16[1,1024,2,256]{3,2,1,0:T(2,128)(2,1)} %param.18) | copy-start | bytes 3145732
  2.2 6.7 %collective-permute-start = (bf16[16,2560]{1,0:T(8,128)(2,1)}, bf16[16,2560]{1,0:T(8,128)(2,1)S(1)}, u32[]{:S(2)}, u32[]{:S(2)}) collective-permute-start(bf16[16,2560]{1,0:T(8,128)(2,1)} %edge_rows.1.edge_hbm), channel_id=1, source_target_pairs={{0,64},{1,65},{2,66},{3,67},{4,68},{5,69},{6,70},{7,71},{8,72},{9,... | collective-permute-start | bytes 245768 | tf_op jit(solution)/shard_map/ppermute | solution.py:499
  8.8 13.4 %copy-start.4 = (bf16[16,2560]{1,0:T(8,128)(2,1)}, bf16[16,2560]{1,0:T(8,128)(2,1)S(1)}, u32[]{:S(2)}) copy-start(bf16[16,2560]{1,0:T(8,128)(2,1)S(1)} %collective-permute-done.got_ref) | copy-start | bytes 245764
  8.8 38.4 %all-to-all-start = ((bf16[64,128,128]{2,1,0:T(8,128)(2,1)}), bf16[64,128,128]{2,1,0:T(8,128)(2,1)S(1)}, u32[]{:S(2)}, u32[]{:S(2)}) async-start(bf16[64,128,128]{2,1,0:T(8,128)(2,1)} %bitcast.29), calls=%async_computation | async-start | bytes 4194304 | tf_op jit(solution)/shard_map/all_to_all | solution.py:502
  32.7 20.6 %collective-permute-start.3 = (bf16[144,1024]{1,0:T(8,128)(2,1)}, bf16[144,1024]{1,0:T(8,128)(2,1)S(1)}, u32[]{:S(2)}, u32[]{:S(2)}) collective-permute-start(bf16[144,1024]{1,0:T(8,128)(2,1)} %get-tuple-element.23.rest_3_), channel_id=1, source_target_pairs={{0,64},{1,65},{2,66},{3,67},{4,68},{5,69},{6,70},{7,71},{8,72},{9,... | collective-permute-start | bytes 884744 | tf_op jit(solution)/shard_map/ppermute | solution.py:514
  44.5 14.7 %collective-permute-start.2 = (bf16[144,1024]{1,0:T(8,128)(2,1)}, bf16[144,1024]{1,0:T(8,128)(2,1)S(1)}, u32[]{:S(2)}, u32[]{:S(2)}) collective-permute-start(bf16[144,1024]{1,0:T(8,128)(2,1)} %get-tuple-element.22.rest_1_), channel_id=1, source_target_pairs={{0,64},{64,0},{1,65},{65,1},{2,66},{66,2},{3,67},{67,3},{4,68},{68... | collective-permute-start | bytes 884744 | tf_op jit(solution)/shard_map/ppermute | solution.py:516
  47.2 1.3 %copy-start = (bf16[64,128,128]{2,1,0:T(8,128)(2,1)}, bf16[64,128,128]{2,1,0:T(8,128)(2,1)S(1)}, u32[]{:S(2)}) copy-start(bf16[64,128,128]{2,1,0:T(8,128)(2,1)S(1)} %all-to-all-done) | copy-start | bytes 6291460
  51.1 13.2 %collective-permute-start.1 = (bf16[128,1024]{1,0:T(8,128)(2,1)}, bf16[128,1024]{1,0:T(8,128)(2,1)S(1)}, u32[]{:S(2)}, u32[]{:S(2)}) collective-permute-start(bf16[128,1024]{1,0:T(8,128)(2,1)} %select_states.1.cached_ref.rest_0_), channel_id=1, source_target_pairs={{0,64},{64,0},{1,65},{65,1},{2,66},{66,2},{3,67},{67,3},{4,68},{68... | collective-permute-start | bytes 786440 | tf_op jit(solution)/shard_map/ppermute | solution.py:521
  53.3 0.7 %copy-start.2 = (bf16[144,1024]{1,0:T(8,128)(2,1)}, bf16[144,1024]{1,0:T(8,128)(2,1)S(1)}, u32[]{:S(2)}) copy-start(bf16[144,1024]{1,0:T(8,128)(2,1)S(1)} %collective-permute-done.3.before_ref.rest_4_) | copy-start | bytes 884740
  59.1 5.1 %copy-start.3 = (bf16[144,1024]{1,0:T(8,128)(2,1)}, bf16[144,1024]{1,0:T(8,128)(2,1)S(1)}, u32[]{:S(2)}) copy-start(bf16[144,1024]{1,0:T(8,128)(2,1)S(1)} %collective-permute-done.2.before_ref.rest_2_) | copy-start | bytes 884740
  64.3 0.7 copy-start.5

commit v3 on v2

--- a/solution.py
+++ b/solution.py
@@ -13,6 +13,10 @@
 LOCAL_ROWS = 256
 MIB = 1 << 20
 VMEM_LIMIT = 56 * MIB
+EDGE_LIMIT = 63 * MIB
+PACK_LIMIT = 61 * MIB
+SELECT_LIMIT = 16 * MIB
+JOIN_LIMIT = 40 * MIB
 F32 = jnp.float32
 BF16 = jnp.bfloat16
 SMEM = pltpu.SMEM
@@ -42,6 +46,14 @@
 
 def iota(shape, dim):
     return lax.broadcasted_iota(jnp.int32, shape, dim)
+
+
+def in_vmem(*values):
+    return tuple(pltpu.with_memory_space_constraint(v, pltpu.VMEM) for v in values)
+
+
+def in_hbm(*values):
+    return tuple(pltpu.with_memory_space_constraint(v, pltpu.HBM) for v in values)
 
 
 def over(v, power_of_two):
@@ -69,7 +81,7 @@
             pl.BlockSpec((16,) + bc.shape[1:], lambda i: (last, 0, 0)),
         ],
         out_specs=pl.BlockSpec(edge, lambda i: (0, 0)),
-        compiler_params=pltpu.CompilerParams(vmem_limit_bytes=VMEM_LIMIT),
+        compiler_params=pltpu.CompilerParams(vmem_limit_bytes=EDGE_LIMIT),
         cost_estimate=pl.CostEstimate(flops=0, bytes_accessed=MIB // 4, transcendentals=0),
         name="edge_rows",
     )(x, bc)
@@ -153,13 +165,24 @@
             pltpu.SemaphoreType.DMA((4,)),
             pltpu.SemaphoreType.DMA,
         ],
-        compiler_params=pltpu.CompilerParams(vmem_limit_bytes=VMEM_LIMIT),
+        compiler_params=pltpu.CompilerParams(vmem_limit_bytes=PACK_LIMIT),
         cost_estimate=pl.CostEstimate(flops=0, bytes_accessed=6 * MIB, transcendentals=0),
         name="pack_states",
     )(slots, pool, edge)
 
 
-def select_kernel(slots_ref, incoming_ref, out_ref, *, slots_dev, held):
+def decay_of(ref, cols):
+    rows = ref[BLK : BLK + 16, cols].astype(F32)
+    return rows[0:1] + rows[1:2] + rows[2:3]
+
+
+def moved(ref, cols, cached):
+    return decay_of(ref, cols) * cached + ref[:BLK, cols].astype(F32)
+
+
+def select_kernel(
+    slots_ref, incoming_ref, mine_ref, theirs_ref, start_ref, sent_ref, *, slots_dev, held
+):
     section_count = lax.axis_size("section")
     mp_count = lax.axis_size("mp")
     peer_count = lax.axis_size("cache") * mp_count
@@ -179,26 +202,37 @@
         two = jnp.concatenate(
             [incoming_ref[index[2 * pair + k]].astype(F32) for k in range(2)], 0
         )
-        out_ref[:, pair * BLK : (pair + 1) * BLK] = two.T.astype(BF16)
-
-
-def select(slots, incoming, quarter, held):
+        cols = slice(pair * BLK, (pair + 1) * BLK)
+        cached = two.T
+
+        @pl.when(lax.axis_index("section") == 0)
+        def _(cols=cols, cached=cached):
+            start_ref[:, cols] = cached.astype(BF16)
+            sent_ref[:, cols] = moved(mine_ref, cols, cached).astype(BF16)
+
+        @pl.when(lax.axis_index("section") == 1)
+        def _(cols=cols, cached=cached):
+            start_ref[:, cols] = moved(theirs_ref, cols, cached).astype(BF16)
+            sent_ref[:, cols] = cached.astype(BF16)
+
+
+def select(slots, incoming, mine, theirs, quarter, held):
     count, head_dim, state_size = incoming.shape
     return pl.pallas_call(
         functools.partial(select_kernel, slots_dev=count, held=held),
-        out_shape=jax.ShapeDtypeStruct((state_size, quarter * head_dim), BF16),
-        in_specs=[pl.BlockSpec(memory_space=SMEM), pl.BlockSpec(memory_space=VMEM)],
-        out_specs=pl.BlockSpec(memory_space=VMEM),
-        compiler_params=pltpu.CompilerParams(vmem_limit_bytes=VMEM_LIMIT),
+        out_shape=[jax.ShapeDtypeStruct((state_size, quarter * head_dim), BF16)] * 2,
+        in_specs=[pl.BlockSpec(memory_space=SMEM)] + [pl.BlockSpec(memory_space=VMEM)] * 3,
+        out_specs=[pl.BlockSpec(memory_space=VMEM)] * 2,
+        compiler_params=pltpu.CompilerParams(vmem_limit_bytes=SELECT_LIMIT),
         cost_estimate=pl.CostEstimate(flops=0, bytes_accessed=3 * MIB, transcendentals=0),
         name="select_states",
-    )(slots, incoming)
+    )(slots, incoming, mine, theirs)
 
 
 def local_kernel(
-    len_ref, x_ref, z_ref, bc_ref, dt_ref, bias_ref, rate_ref, got_ref,
+    group_ref, len_ref, x_ref, z_ref, bc_ref, dt_ref, bias_ref, rate_ref, got_x_ref, got_bc_ref,
     tail_x_ref, tail_bc_ref, tap_x_ref, off_x_ref, tap_bc_ref, off_bc_ref, *rest,
-    group, blocks, head_dim,
+    blocks, head_dim,
 ):
     a_ref, b_ref, c_ref, t_ref, spread, factors, behind, state, decay = rest[-9:]
     step = pl.program_id(0)
@@ -207,21 +241,22 @@
     state_size = bc_ref.shape[1] // 2
     per_step = x_ref.shape[0] // BLK
     chunk = 256
-    here = slice(group * heads, (group + 1) * heads)
+    is_last = group_ref[0] == 1
+
+    def of_group(low, high):
+        return jnp.where(is_last, high, low)
 
     @pl.when(step == 0)
     def _():
         section = lax.axis_index("section")
-        got_x = got_ref[:, group * width : (group + 1) * width].astype(F32)[8:]
-        at = lax.axis_size("section") * width + group * 2 * state_size
-        got_bc = got_ref[:, at : at + 2 * state_size].astype(F32)[8:]
-        behind[:, :width] = got_x
-        behind[:, width:] = got_bc
+        behind[:, :width] = got_x_ref[...].astype(F32)[8:]
+        behind[:, width:] = got_bc_ref[...].astype(F32)[8:]
 
         @pl.when(section == 0)
         def _():
-            behind[5:8, :width] = tail_x_ref[:, group * width : (group + 1) * width].astype(F32)
-            behind[5:8, width:] = tail_bc_ref[:, group, :].astype(F32)
+            behind[5:8, :width] = tail_x_ref[...].astype(F32)
+            tail = tail_bc_ref[...].astype(F32)
+            behind[5:8, width:] = of_group(tail[:, 0, :], tail[:, 1, :])
 
         state[...] = jnp.zeros_like(state)
         decay[...] = jnp.ones_like(decay)
@@ -231,23 +266,22 @@
             spread[:, at : at + BLK] = jnp.where(
                 (iota(shape, 0) & (heads - 1)) == head, 1.0, 0.0
             ).astype(BF16)
-        raw = dt_ref[here, :].astype(F32)
+        raw = dt_ref[...].astype(F32)
         stacked = lambda v: jnp.concatenate([v] * blocks, 0)
         value = jnp.concatenate([raw[:, k * BLK : (k + 1) * BLK] for k in range(blocks)], 0)
         flat = jnp.concatenate(
             [bias_ref[...], rate_ref[...], jnp.zeros((1, BLK - 2 * bias_ref.shape[1]), F32)], 1
         )
         turned = jnp.broadcast_to(flat, (BLK, BLK)).T
-        value = value + stacked(turned[here])
+        column = lambda at: of_group(turned[at : at + heads], turned[at + heads : at + 2 * heads])
+        value = value + stacked(column(0))
         soft = jnp.maximum(value, 0.0) + jnp.log1p(jnp.exp(-jnp.abs(value)))
         shape = value.shape
         position = (
             section * (blocks * BLK) + over(iota(shape, 0), heads) * BLK + iota(shape, 1)
         )
         steps = jnp.where(position < len_ref[0], soft, 0.0)
-        log_decay = -steps * stacked(
-            turned[bias_ref.shape[1] + group * heads : bias_ref.shape[1] + (group + 1) * heads]
-        )
+        log_decay = -steps * stacked(column(bias_ref.shape[1]))
         upper = jnp.where(iota((BLK, BLK), 0) <= iota((BLK, BLK), 1), 1.0, 0.0).astype(BF16)
         cum_log = sum(dot(part, upper) for part in split_three(log_decay))
         owner = over(iota((BLK, BLK), 1), heads)
@@ -274,7 +308,8 @@
         rows = slice(sub * BLK, (sub + 1) * BLK)
         mixed = conv(
             bc_ref, 0, 2 * state_size, width,
-            tap_bc_ref[:, group, :], off_bc_ref[group : group + 1, :],
+            of_group(tap_bc_ref[:, 0, :], tap_bc_ref[:, 1, :]),
+            of_group(off_bc_ref[0:1, :], off_bc_ref[1:2, :]),
         )
         c_block = mixed[:, state_size:].astype(BF16)
         b_turned = mixed[:, :state_size].T.astype(BF16)
@@ -313,42 +348,50 @@
     seg_len, channels = x.shape
     blocks = seg_len // BLK
     width = channels // groups
-    head_dim = channels // dt.shape[0]
+    heads = dt.shape[0] // groups
     pair = bc.shape[1] // groups
-    body = functools.partial(local_kernel, group=group, blocks=blocks, head_dim=head_dim)
-    by_block = lambda size: pl.BlockSpec((LOCAL_ROWS, size), lambda i: (i, group))
-    whole = lambda shape: pl.BlockSpec(shape, lambda i: (0,) * len(shape))
-    column = lambda size: pl.BlockSpec((size, width), lambda i: (0, group))
+    ahead = channels // pair
+    body = functools.partial(local_kernel, blocks=blocks, head_dim=width // heads)
+    by_block = lambda size: pl.BlockSpec((LOCAL_ROWS, size), lambda i, at: (i, at[0]))
+    whole = lambda shape: pl.BlockSpec(shape, lambda i, at: (0,) * len(shape))
+    column = lambda size: pl.BlockSpec((size, width), lambda i, at: (0, at[0]))
     shapes = (
         jax.ShapeDtypeStruct((seg_len, channels), BF16),
         jax.ShapeDtypeStruct((seg_len, channels), BF16),
         jax.ShapeDtypeStruct((seg_len, groups * pair // 2), BF16),
-        jax.ShapeDtypeStruct((BLK + 16, width), BF16),
+        VMEM((BLK + 16, width), BF16),
     )
     operands = (
-        length, x, z, bc, dt, bias, rate, received, tail_x, tail_bc, tap_x, off_x, tap_bc, off_bc,
+        group, length, x, z, bc, dt, bias, rate, received, received,
+        tail_x, tail_bc, tap_x, off_x, tap_bc, off_bc,
     )
     return pl.pallas_call(
         body,
         out_shape=shapes,
-        grid=(seg_len // LOCAL_ROWS,),
-        in_specs=[
-            pl.BlockSpec(memory_space=SMEM),
-            by_block(width), by_block(width), by_block(pair),
-            whole(dt.shape), whole(bias.shape), whole(rate.shape), whole(received.shape),
-            whole(tail_x.shape), whole(tail_bc.shape),
-            column(tap_x.shape[0]), column(1), whole(tap_bc.shape), whole(off_bc.shape),
-        ] + [pl.BlockSpec(memory_space=pl.ANY)] * len(into),
-        out_specs=(
-            by_block(width), by_block(width), by_block(pair // 2), whole((BLK + 16, width)),
+        grid_spec=pltpu.PrefetchScalarGridSpec(
+            num_scalar_prefetch=1,
+            grid=(seg_len // LOCAL_ROWS,),
+            in_specs=[
+                pl.BlockSpec(memory_space=SMEM),
+                by_block(width), by_block(width), by_block(pair),
+                pl.BlockSpec((heads, seg_len), lambda i, at: (at[0], 0)),
+                whole(bias.shape), whole(rate.shape),
+                column(received.shape[0]),
+                pl.BlockSpec((received.shape[0], pair), lambda i, at: (0, ahead + at[0])),
+                column(tail_x.shape[0]), whole(tail_bc.shape),
+                column(tap_x.shape[0]), column(1), whole(tap_bc.shape), whole(off_bc.shape),
+            ] + [pl.BlockSpec(memory_space=pl.ANY)] * len(into),
+            out_specs=(
+                by_block(width), by_block(width), by_block(pair // 2), whole((BLK + 16, width)),
+            ),
+            scratch_shapes=[
+                VMEM((2 * BLK, width), BF16),
+                VMEM((blocks, 2 * BLK, 2 * BLK), BF16),
+                VMEM((8, width + pair), F32),
+                VMEM((BLK, width), F32),
+                VMEM((8, width), F32),
+            ],
         ),
-        scratch_shapes=[
-            VMEM((2 * BLK, width), BF16),
-            VMEM((blocks, 2 * BLK, 2 * BLK), BF16),
-            VMEM((8, width + pair), F32),
-            VMEM((BLK, width), F32),
-            VMEM((8, width), F32),
-        ],
         input_output_aliases={len(operands) + k: k for k in range(len(into))},
         compiler_params=pltpu.CompilerParams(vmem_limit_bytes=VMEM_LIMIT),
         cost_estimate=pl.CostEstimate(
@@ -359,51 +402,24 @@
     )(*operands, *into)
 
 
-def decay_of(ref, cols):
-    rows = ref[BLK : BLK + 16, cols].astype(F32)
-    return rows[0:1] + rows[1:2] + rows[2:3]
-
-
-def moved(ref, cols, cached):
-    return decay_of(ref, cols) * cached + ref[:BLK, cols].astype(F32)
-
-
-def join_kernel(
-    group_ref, len_ref, a_ref, b_ref, c_ref, cached_ref, before_ref, gain_ref, *rest, ending
-):
+def join_kernel(group_ref, len_ref, a_ref, b_ref, c_ref, start, gain_ref, *rest, ending):
     if ending:
-        own_ref, mine0_ref, theirs0_ref, mine1_ref, theirs1_ref, _ = rest[:6]
-        out_ref, final_ref, start, gated = rest[6:]
+        sent_ref, mine_ref, theirs_ref, out_ref, final_ref, gated = rest
     else:
-        out_ref, start, gated = rest
+        out_ref, gated = rest[1:]
     step = pl.program_id(0)
     section = lax.axis_index("section")
     width = a_ref.shape[1]
     chunk = 256
 
-    @pl.when(step == 0)
-    def _():
-        @pl.when(section == 0)
-        def _():
-            start[...] = cached_ref[...]
-
-        @pl.when(section == 1)
-        def _():
-            for at in range(0, width, chunk):
-                cols = slice(at, at + chunk)
-                start[:, cols] = moved(before_ref, cols, cached_ref[:, cols].astype(F32)).astype(BF16)
-
     if ending:
-        last = pl.num_programs(0) - 1
-        orders = ((mine0_ref, theirs0_ref), (theirs1_ref, mine1_ref))
-        for place, (early_ref, late_ref) in enumerate(orders):
-
-            @pl.when((step == last) & (section == place))
-            def _(early_ref=early_ref, late_ref=late_ref):
+        for place, (from_ref, late_ref) in enumerate(((sent_ref, theirs_ref), (start, mine_ref))):
+
+            @pl.when((step == 0) & (section == place))
+            def _(from_ref=from_ref, late_ref=late_ref):
                 for at in range(0, width, BLK):
                     cols = slice(at, at + BLK)
-                    middle = moved(early_ref, cols, own_ref[:, cols].astype(F32))
-                    final_ref[cols, :] = moved(late_ref, cols, middle).T
+                    final_ref[cols, :] = moved(late_ref, cols, from_ref[:, cols].astype(F32)).T
 
     size = a_ref.shape[0]
     position = (section * pl.num_programs(0) + step) * size + iota((size, 1), 0)
@@ -425,21 +441,17 @@
         out_ref[:, cols] = (gated[:, cols] * scale * gain_ref[:, cols]).astype(BF16)
 
 
-def join_part(group, groups, length, a, b, c, cached, before, gain, ending=()):
+def join_part(group, groups, length, a, b, c, start, gain, ending=(), into=()):
     seg_len, channels = a.shape
     width = channels // groups
     by_block = lambda size: pl.BlockSpec((JOIN_ROWS, size), lambda i, at: (i, at[0]))
     whole = lambda shape: pl.BlockSpec(shape, lambda i, at: (0,) * len(shape))
     out_shape = [jax.ShapeDtypeStruct((seg_len, channels), BF16)]
     out_specs = [by_block(width)]
-    extra = []
-    aliases = {}
     if ending:
-        final_shape = (cached.shape[1], cached.shape[0])
+        final_shape = (start.shape[1], start.shape[0])
         out_shape.append(jax.ShapeDtypeStruct(final_shape, F32))
         out_specs.append(whole(final_shape))
-        extra = [whole(v.shape) for v in ending[:-1]] + [pl.BlockSpec(memory_space=pl.ANY)]
-        aliases = {8 + len(ending) - 1: 0}
     return pl.pallas_call(
         functools.partial(join_kernel, ending=bool(ending)),
         out_shape=out_shape,
@@ -449,19 +461,21 @@
             in_specs=[
                 pl.BlockSpec(memory_space=SMEM),
                 by_block(width), by_block(width), by_block(c.shape[1] // groups),
-                whole(cached.shape), whole(before.shape),
+                pl.BlockSpec(memory_space=VMEM),
                 pl.BlockSpec((1, width), lambda i, at: (0, at[0])),
-            ] + extra,
+            ]
+            + [pl.BlockSpec(memory_space=VMEM)] * len(ending)
+            + [pl.BlockSpec(memory_space=pl.ANY)] * len(into),
             out_specs=out_specs,
-            scratch_shapes=[VMEM((BLK, width), BF16), VMEM((JOIN_ROWS, width), F32)],
+            scratch_shapes=[VMEM((JOIN_ROWS, width), F32)],
         ),
-        input_output_aliases=aliases,
-        compiler_params=pltpu.CompilerParams(vmem_limit_bytes=VMEM_LIMIT),
+        input_output_aliases={7: 0} if into else {},
+        compiler_params=pltpu.CompilerParams(vmem_limit_bytes=JOIN_LIMIT),
         cost_estimate=pl.CostEstimate(
             flops=2 * seg_len * width * BLK, bytes_accessed=7 * MIB, transcendentals=0
         ),
         name="join_blocks",
-    )(group, length, a, b, c, cached, before, gain, *ending)
+    )(group, length, a, b, c, start, gain, *ending, *into)
 
 
 def body(
@@ -510,20 +524,23 @@
         conv_w_x, conv_b_x[None], conv_w_bc, conv_b_bc,
     )
     shared = (new_len, x_in[0], z_in[0], bc2, dt_in[0].T, params, received)
-    a, b, c, mine1 = local_part(1, groups, *shared, ())
-    theirs1 = lax.ppermute(mine1, "section", forth)
-    a, b, c, mine0 = local_part(0, groups, *shared, (a, b, c))
-    theirs0 = lax.ppermute(mine0, "section", swap)
-
-    own = select(
-        block_slots, incoming.reshape(peer_count * held, head_dim, state_size), quarter, held
-    )
-    other = lax.ppermute(own, "section", swap)
+    far, near = 1 - section[None], section[None]
+    a, b, c, leaving = local_part(far, groups, *shared, ())
+    theirs = lax.ppermute(leaving, "section", swap)
+    a, b, c, mine = local_part(near, groups, *shared, (a, b, c))
+
+    start, sent = select(
+        block_slots, incoming.reshape(peer_count * held, head_dim, state_size),
+        *in_vmem(mine, theirs), quarter, held,
+    )
+    other = lax.ppermute(sent, "section", swap)
     gain = norm_gain[None]
-    (gated,) = join_part(section[None], groups, new_len, a, b, c, own, theirs1, gain)
     gated, final = join_part(
-        1 - section[None], groups, new_len, a, b, c, other, theirs0, gain,
-        (own, mine0, theirs0, mine1, theirs1, gated),
+        near, groups, new_len, *in_hbm(a, b, c), *in_vmem(start), gain,
+        in_vmem(sent, mine, theirs),
+    )
+    (gated,) = join_part(
+        far, groups, new_len, *in_hbm(a, b, c), *in_vmem(other), gain, into=in_hbm(gated)
     )
     return (
         gated[None],

time: 71 us -> 66.7 us (0.939)
  waiting for transfers between devices: 5.8 us -> 10.5 us
  starting transfers between devices: 19.1 us -> 15.4 us
  local copies, waits for them, and re-layouts: 3.97 us -> 1.3 us
  Pallas kernels: 40.3 us -> 37.7 us
    ppermute x3 -> x2, waiting for transfers between devices: 5.53 us -> 10.2 us  [the longest x1 6.84 us: body(): theirs = lax.ppermute(leaving, 'section', swap)]
    ppermute x3 -> x2, starting transfers between devices: 6.2 us -> 2.56 us  [the longest x1 2.47 us: body(): theirs = lax.ppermute(leaving, 'section', swap)]
    unnamed x13 -> x9, local copies, waits for them, and re-layouts: 3.97 us -> 1.3 us
    pallas_call x2, Pallas kernels: 10.3 us -> 8.6 us  [join_part(): pl.pallas_call(functools.partial(join_kernel, ending=bool(ending)), out_s...]
    pallas_call x1, Pallas kernels: 2.57 us -> 1.81 us  [select(): pl.pallas_call(functools.partial(select_kernel, slots_dev=count, held=hel...]
  transfers between devices with their start and end apart: 5 -> 4, of which waited for: 3 -> 3; matrix products, arithmetic and copies ran while one was open for 2% -> 2% of each run, Pallas kernels for 47% -> 46%
where the time goes in v3:
time: 66.7 us; the launch traced here: 66.3 us
  Pallas kernels  37.7 us (57%)
  starting transfers between devices  15.4 us (23%)
  waiting for transfers between devices  10.5 us (16%)
  between operations  1.34 us (2%)
  local copies, waits for them, and re-layouts  1.3 us (2%)
    pallas_call x2, Pallas kernels, local_part(): pl.pallas_call(body, out_shape=shapes, grid_spec=pltpu.PrefetchScalarGrid...  20.8 us
    all_to_all x1, starting transfers between devices, body(): lax.all_to_all(outgoing.reshape(peer_count, held * head_dim, state_size),...  11.5 us
    pallas_call x2, Pallas kernels, join_part(): pl.pallas_call(functools.partial(join_kernel, ending=bool(ending)), out_s...  8.6 us
    ppermute x1, waiting for transfers between devices, body(): theirs = lax.ppermute(leaving, 'section', swap)  6.84 us
    pallas_call x1, Pallas kernels, pack(): pl.pallas_call(pack_kernel, out_shape=jax.ShapeDtypeStruct(pool.shape, BF...  4.97 us
    ppermute x1, waiting for transfers between devices, body(): other = lax.ppermute(sent, 'section', swap)  3.38 us
    ppermute x1, starting transfers between devices, body(): theirs = lax.ppermute(leaving, 'section', swap)  2.47 us
    pallas_call x1, Pallas kernels, select(): pl.pallas_call(functools.partial(select_kernel, slots_dev=count, held=hel...  1.81 us
  transfers between devices with their start and end apart: 4, of which 3 were waited for; matrix products, arithmetic and copies ran while one was open for 2% of the time, Pallas kernels for 46%

profile of v3, /device:TPU:6, one launch (start us, length us, event | category | flops | bytes accessed | tf_op | source)
XLA Modules:
  0.0 66.3 jit_solution(13311589977109894386)
XLA Ops:
  0.6 1.5 %edge_rows.1.edge_hbm = bf16[16,2560]{1,0:T(8,128)(2,1)} custom-call(bf16[1024,2048]{1,0:T(8,128)(2,1)} %bitcast.23, bf16[1024,2,256]{2,1,0:T(2,128)(2,1)} %bitcast.31), custom_call_target="tpu_custom_call" | custom-call | bytes 262144 | tf_op jit(solution)/shard_map/edge_rows/pallas_call | solution.py:75
  2.2 0.0 copy-start.2
  2.2 1.4 %collective-permute-start = (bf16[16,2560]{1,0:T(8,128)(2,1)}, bf16[16,2560]{1,0:T(8,128)(2,1)S(1)}, u32[]{:S(2)}, u32[]{:S(2)}) collective-permute-start(bf16[16,2560]{1,0:T(8,128)(2,1)} %edge_rows.1.edge_hbm), channel_id=1, source_target_pairs={{0,64},{1,65},{2,66},{3,67},{4,68},{5,69},{6,70},{7,71},{8,72},{9,... | collective-permute-start | bytes 245768 | tf_op jit(solution)/shard_map/ppermute | solution.py:513
  3.6 5.0 %pack_states.1 = bf16[128,64,128]{2,1,0:T(8,128)(2,1)} custom-call(s32[16,128]{1,0:T(8,128)} %slots_ref.3, f32[128,64,128]{2,1,0:T(8,128)} %pool_hbm.1, bf16[16,2560]{1,0:T(8,128)(2,1)} %edge_rows.1.edge_hbm), custom_call_target="tpu_custom_call" | custom-call | bytes 6291456 | tf_op jit(solution)/shard_map/pack_states/pallas_call | solution.py:151
  8.6 0.3 collective-permute-done.got_x_ref.got_bc_ref
  8.8 0.0 copy-start.3
  8.8 11.5 %all-to-all-start = ((bf16[64,128,128]{2,1,0:T(8,128)(2,1)}), bf16[64,128,128]{2,1,0:T(8,128)(2,1)S(1)}, u32[]{:S(2)}, u32[]{:S(2)}) async-start(bf16[64,128,128]{2,1,0:T(8,128)(2,1)} %bitcast.30), calls=%async_computation | async-start | bytes 4194304 | tf_op jit(solution)/shard_map/all_to_all | solution.py:516
  21.0 0.0 copy-done.2
  21.0 1.3 %copy.22 = bf16[128,8,2,256]{3,1,2,0:T(8,128)(2,1)} copy(bf16[128,8,2,256]{3,2,1,0:T(2,128)(2,1)S(1)} %bitcast.32) | data formatting | bytes 2097152
  22.3 0.0 copy-done.3
  22.3 10.4 %local_blocks.2 = (bf16[1024,2048]{1,0:T(8,128)(2,1)}, bf16[1024,2048]{1,0:T(8,128)(2,1)}, bf16[1024,256]{1,0:T(8,128)(2,1)}, bf16[144,1024]{1,0:T(8,128)(2,1)S(1)}) custom-call(s32[1]{0:T(128)S(6)} %sub.3.group_ref, s32[1]{0:T(128)S(6)} %copy.27.len_ref, bf16[1024,2048]{1,0:T(8,128)(2,1)} %bitcast.24, bf16[1024,2048]{1,0:T(8,128)(2,1)} %bitcast.26, ...), custom_call_target="tpu_custom_call" | custom-call | flops 2147483648 | bytes 10485760 | tf_op jit(solution)/shard_map/local_blocks/pallas_call | solution.py:368
  32.7 2.5 %collective-permute-start.1 = (bf16[144,1024]{1,0:T(8,128)(2,1)S(1)}, bf16[144,1024]{1,0:T(8,128)(2,1)S(1)}, u32[]{:S(2)}, u32[]{:S(2)}) collective-permute-start(bf16[144,1024]{1,0:T(8,128)(2,1)S(1)} %get-tuple-element.25), channel_id=1, source_target_pairs={{0,64},{64,0},{1,65},{65,1},{2,66},{66,2},{3,67},{67,3},{4,68},{68... | collective-permute-start | bytes 884744 | tf_op jit(solution)/shard_map/ppermute | solution.py:529
  35.1 0.0 copy-start
  35.1 0.0 copy-start.1
  35.1 10.4 %local_blocks.3 = (bf16[1024,2048]{1,0:T(8,128)(2,1)}, bf16[1024,2048]{1,0:T(8,128)(2,1)}, bf16[1024,256]{1,0:T(8,128)(2,1)}, bf16[144,1024]{1,0:T(8,128)(2,1)S(1)}) custom-call(s32[1]{0:T(128)} %bitcast.group_ref, s32[1]{0:T(128)S(6)} %copy.27.len_ref, bf16[1024,2048]{1,0:T(8,128)(2,1)} %bitcast.25, ...), custom_call_target="tpu_custom_call", output_to_operand_aliasing={{0}: (16, {}), {1}: (17, {}), {2}: (18, {})} | custom-call | flops 2147483648 | bytes 10485760 | tf_op jit(solution)/shard_map/local_blocks/pallas_call | solution.py:368
  45.5 6.8 %collective-permute-done.1.theirs_ref.rest_2_ = bf16[144,1024]{1,0:T(8,128)(2,1)S(1)} collective-permute-done((bf16[144,1024]{1,0:T(8,128)(2,1)S(1)}, bf16[144,1024]{1,0:T(8,128)(2,1)S(1)}, u32[]{:S(2)}, u32[]{:S(2)}) %collective-permute-start.1) | collective-permute-done | bytes 294944 | tf_op jit(solution)/shard_map/ppermute | solution.py:529
  52.3 0.0 all-to-all-done
  52.3 0.0 copy-done
  52.4 1.8 %select_states.1 = (bf16[128,1024]{1,0:T(8,128)(2,1)S(1)}, bf16[128,1024]{1,0:T(8,128)(2,1)S(1)}) custom-call(s32[16,128]{1,0:T(8,128)S(1)} %copy-done, bf16[128,64,128]{2,1,0:T(8,128)(2,1)S(1)} %bitcast.20, bf16[144,1024]{1,0:T(8,128)(2,1)S(1)} %get-tuple-element.24.mine_ref.rest_1_, bf16[144,1024]{1,0:T(8,128)(2,1)S(1)} %collective-permute-done.1.theirs_ref.rest_2_), custom_call_target="tpu_custom_call" | custom-call | bytes 3145728 | tf_op jit(solution)/shard_map/select_states/pallas_call | solution.py:221
  54.2 0.1 collective-permute-start.2
  54.3 0.0 copy-done.1
  54.3 4.4 %join_blocks.2 = (bf16[1024,2048]{1,0:T(8,128)(2,1)}, f32[1024,128]{1,0:T(8,128)}) custom-call(s32[1]{0:T(128)} %bitcast.group_ref, s32[1]{0:T(128)S(6)} %copy.27.len_ref, bf16[1024,2048]{1,0:T(8,128)(2,1)} %get-tuple-element.20.a_ref, bf16[1024,2048]{1,0:T(8,128)(2,1)} %get-tuple-element.21.b_ref, bf16[1024,256]{1,0:T(8,128)(2,1)} %get-tuple-element.22.c_ref, ...), custom_call_target="tpu_custom_call" | custom-call | flops 268435456 | bytes 7340032 | tf_op jit(solution)/shard_map/join_blocks/pallas_call | solution.py:455
  58.7 3.4 %collective-permute-done.2.start = bf16[128,1024]{1,0:T(8,128)(2,1)S(1)} collective-permute-done((bf16[128,1024]{1,0:T(8,128)(2,1)S(1)}, bf16[128,1024]{1,0:T(8,128)(2,1)S(1)}, u32[]{:S(2)}, u32[]{:S(2)}) %collective-permute-start.2) | collective-permute-done | bytes 262176 | tf_op jit(solution)/shard_map/ppermute | solution.py:536
  62.1 4.2 %join_blocks.3 = bf16[1024,2048]{1,0:T(8,128)(2,1)} custom-call(s32[1]{0:T(128)S(6)} %sub.3.group_ref, s32[1]{0:T(128)S(6)} %copy.27.len_ref, bf16[1024,2048]{1,0:T(8,128)(2,1)} %get-tuple-element.20.a_ref, bf16[1024,2048]{1,0:T(8,128)(2,1)} %get-tuple-element.21.b_ref, bf16[1024,256]{1,0:T(8,128)(2,1)} %get-tuple-element.22.c_ref, ...), custom_call_target="tpu_custom_call", output_to_operand_aliasing={{}: (7, {})} | custom-call | flops 268435456 | bytes 7340032 | tf_op jit(solution)/shard_map/join_blocks/pallas_call | solution.py:455
Async XLA Ops:
  2.2 18.8 %copy-start.2 = (bf16[1,1024,2,256]{3,2,1,0:T(2,128)(2,1)S(1)}, bf16[1,1024,2,256]{3,2,1,0:T(2,128)(2,1)}, u32[]{:S(2)}) copy-start(bf16[1,1024,2,256]{3,2,1,0:T(2,128)(2,1)} %param.18) | copy-start | bytes 3145732
  2.2 6.7 %collective-permute-start = (bf16[16,2560]{1,0:T(8,128)(2,1)}, bf16[16,2560]{1,0:T(8,128)(2,1)S(1)}, u32[]{:S(2)}, u32[]{:S(2)}) collective-permute-start(bf16[16,2560]{1,0:T(8,128)(2,1)} %edge_rows.1.edge_hbm), channel_id=1, source_target_pairs={{0,64},{1,65},{2,66},{3,67},{4,68},{5,69},{6,70},{7,71},{8,72},{9,... | collective-permute-start | bytes 245768 | tf_op jit(solution)/shard_map/ppermute | solution.py:513
  8.8 13.4 %copy-start.3 = (bf16[16,2560]{1,0:T(8,128)(2,1)}, bf16[16,2560]{1,0:T(8,128)(2,1)S(1)}, u32[]{:S(2)}) copy-start(bf16[16,2560]{1,0:T(8,128)(2,1)S(1)} %collective-permute-done.got_x_ref.got_bc_ref) | copy-start | bytes 245764
  8.8 43.5 %all-to-all-start = ((bf16[64,128,128]{2,1,0:T(8,128)(2,1)}), bf16[64,128,128]{2,1,0:T(8,128)(2,1)S(1)}, u32[]{:S(2)}, u32[]{:S(2)}) async-start(bf16[64,128,128]{2,1,0:T(8,128)(2,1)} %bitcast.30), calls=%async_computation | async-start | bytes 4194304 | tf_op jit(solution)/shard_map/all_to_all | solution.py:516
  32.7 19.7 %collective-permute-start.1 = (bf16[144,1024]{1,0:T(8,128)(2,1)S(1)}, bf16[144,1024]{1,0:T(8,128)(2,1)S(1)}, u32[]{:S(2)}, u32[]{:S(2)}) collective-permute-start(bf16[144,1024]{1,0:T(8,128)(2,1)S(1)} %get-tuple-element.25), channel_id=1, source_target_pairs={{0,64},{64,0},{1,65},{65,1},{2,66},{66,2},{3,67},{67,3},{4,68},{68... | collective-permute-start | bytes 884744 | tf_op jit(solution)/shard_map/ppermute | solution.py:529
  35.1 17.2 %copy-start = (s32[16,128]{1,0:T(8,128)S(1)}, s32[16,128]{1,0:T(8,128)}, u32[]{:S(2)}) copy-start(s32[16,128]{1,0:T(8,128)} %slots_ref.3) | copy-start | bytes 24580
  35.1 19.1 %copy-start.1 = (f32[2048]{0:T(1024)S(1)}, f32[2048]{0:T(1024)}, u32[]{:S(2)}) copy-start(f32[2048]{0:T(1024)} %param.28) | copy-start | bytes 24580
  54.2 7.9 %collective-permute-start.2 = (bf16[128,1024]{1,0:T(8,128)(2,1)S(1)}, bf16[128,1024]{1,0:T(8,128)(2,1)S(1)}, u32[]{:S(2)}, u32[]{:S(2)}) collective-permute-start(bf16[128,1024]{1,0:T(8,128)(2,1)S(1)} %get-tuple-element.26.rest_0_), channel_id=1, source_target_pairs={{0,64},{64,0},{1,65},{65,1},{2,66},{66,2},{3,67},{67,3},{4,68},{68... | collective-permute-start | bytes 786440 | tf_op jit(solution)/shard_map/ppermute | solution.py:536

commit v4 on v3

--- a/solution.py
+++ b/solution.py
@@ -404,13 +404,29 @@
 
 def join_kernel(group_ref, len_ref, a_ref, b_ref, c_ref, start, gain_ref, *rest, ending):
     if ending:
-        sent_ref, mine_ref, theirs_ref, out_ref, final_ref, gated = rest
+        sent_ref, mine_ref, theirs_ref, *sources = rest[:6]
+        out_ref, final_ref, *handed = rest[6:11]
+        gated, sems = rest[11:]
     else:
         out_ref, gated = rest[1:]
     step = pl.program_id(0)
     section = lax.axis_index("section")
-    width = a_ref.shape[1]
+    size, width = out_ref.shape
     chunk = 256
+    copies = []
+    if ending:
+        rows = slice(None)
+        for at, (source, target) in enumerate(zip(sources, handed)):
+            count = target.shape[1]
+            cols = pl.ds(pl.multiple_of((1 - section) * count, BLK), count)
+            copies.append(pltpu.make_async_copy(source.at[:, cols], target, sems.at[at]))
+
+        @pl.when(step == 0)
+        def _():
+            for copy in copies:
+                copy.start()
+    else:
+        rows = pl.ds(pl.multiple_of(step * size, size), size)
 
     if ending:
         for place, (from_ref, late_ref) in enumerate(((sent_ref, theirs_ref), (start, mine_ref))):
@@ -421,15 +437,14 @@
                     cols = slice(at, at + BLK)
                     final_ref[cols, :] = moved(late_ref, cols, from_ref[:, cols].astype(F32)).T
 
-    size = a_ref.shape[0]
     position = (section * pl.num_programs(0) + step) * size + iota((size, 1), 0)
     live = (position < len_ref[0]).astype(F32)
-    c_block = c_ref[...]
+    c_block = c_ref[rows, :]
     squares = jnp.zeros((size, BLK), F32)
     for at in range(0, width, chunk):
         cols = slice(at, at + chunk)
         inter = dot(c_block, start[:, cols])
-        value = a_ref[:, cols].astype(F32) + b_ref[:, cols].astype(F32) * inter
+        value = a_ref[rows, cols].astype(F32) + b_ref[rows, cols].astype(F32) * inter
         gated[:, cols] = value
         square = value * value
         for k in range(chunk // BLK):
@@ -440,11 +455,23 @@
         cols = slice(at, at + chunk)
         out_ref[:, cols] = (gated[:, cols] * scale * gain_ref[:, cols]).astype(BF16)
 
+    if ending:
+
+        @pl.when(step == pl.num_programs(0) - 1)
+        def _():
+            for copy in copies:
+                copy.wait()
+
 
 def join_part(group, groups, length, a, b, c, start, gain, ending=(), into=()):
-    seg_len, channels = a.shape
-    width = channels // groups
+    seg_len = a.shape[0]
+    state_size, width = start.shape
+    channels = groups * width
     by_block = lambda size: pl.BlockSpec((JOIN_ROWS, size), lambda i, at: (i, at[0]))
+    kept = pl.BlockSpec(memory_space=VMEM)
+    held = [by_block(width), by_block(width), by_block(state_size)] if ending else [kept] * 3
+    scratch = [VMEM((JOIN_ROWS, width), F32)]
+    extra = [kept] * len(ending)
     whole = lambda shape: pl.BlockSpec(shape, lambda i, at: (0,) * len(shape))
     out_shape = [jax.ShapeDtypeStruct((seg_len, channels), BF16)]
     out_specs = [by_block(width)]
@@ -452,6 +479,11 @@
         final_shape = (start.shape[1], start.shape[0])
         out_shape.append(jax.ShapeDtypeStruct(final_shape, F32))
         out_specs.append(whole(final_shape))
+        out_shape += [VMEM((seg_len, count), BF16) for count in (width, width, state_size)]
+        out_specs += [kept] * 3
+        scratch.append(pltpu.SemaphoreType.DMA((3,)))
+        extra += [pl.BlockSpec(memory_space=pl.ANY)] * 3
+        ending = (*ending, a, b, c)
     return pl.pallas_call(
         functools.partial(join_kernel, ending=bool(ending)),
         out_shape=out_shape,
@@ -460,14 +492,14 @@
             grid=(seg_len // JOIN_ROWS,),
             in_specs=[
                 pl.BlockSpec(memory_space=SMEM),
-                by_block(width), by_block(width), by_block(c.shape[1] // groups),
-                pl.BlockSpec(memory_space=VMEM),
+                *held,
+                kept,
                 pl.BlockSpec((1, width), lambda i, at: (0, at[0])),
             ]
-            + [pl.BlockSpec(memory_space=VMEM)] * len(ending)
+            + extra
             + [pl.BlockSpec(memory_space=pl.ANY)] * len(into),
             out_specs=out_specs,
-            scratch_shapes=[VMEM((JOIN_ROWS, width), F32)],
+            scratch_shapes=scratch,
         ),
         input_output_aliases={7: 0} if into else {},
         compiler_params=pltpu.CompilerParams(vmem_limit_bytes=JOIN_LIMIT),
@@ -535,12 +567,12 @@
     )
     other = lax.ppermute(sent, "section", swap)
     gain = norm_gain[None]
-    gated, final = join_part(
+    gated, final, *parcel = join_part(
         near, groups, new_len, *in_hbm(a, b, c), *in_vmem(start), gain,
         in_vmem(sent, mine, theirs),
     )
     (gated,) = join_part(
-        far, groups, new_len, *in_hbm(a, b, c), *in_vmem(other), gain, into=in_hbm(gated)
+        far, groups, new_len, *in_vmem(*parcel), *in_vmem(other), gain, into=in_hbm(gated)
     )
     return (
         gated[None],

time: 66.7 us -> 65.1 us (0.976)
  waiting for transfers between devices: 10.5 us -> 9.4 us
    ppermute x1, waiting for transfers between devices: 3.38 us -> 2.3 us  [body(): other = lax.ppermute(sent, 'section', swap)]
  transfers between devices with their start and end apart: 4 -> 4, of which waited for: 3 -> 3; matrix products, arithmetic and copies ran while one was open for 2% -> 2% of each run, Pallas kernels for 46% -> 48%
where the time goes in v4:
time: 65.1 us; the launch traced here: 64.7 us
  Pallas kernels  37.2 us (57%)
  starting transfers between devices  15.4 us (24%)
  waiting for transfers between devices  9.4 us (14%)
  between operations  1.35 us (2%)
  local copies, waits for them, and re-layouts  1.3 us (2%)
    pallas_call x2, Pallas kernels, local_part(): pl.pallas_call(body, out_shape=shapes, grid_spec=pltpu.PrefetchScalarGrid...  20.8 us
    all_to_all x1, starting transfers between devices, body(): lax.all_to_all(outgoing.reshape(peer_count, held * head_dim, state_size),...  11.5 us
    pallas_call x2, Pallas kernels, join_part(): pl.pallas_call(functools.partial(join_kernel, ending=bool(ending)), out_s...  8.16 us
    ppermute x1, waiting for transfers between devices, body(): theirs = lax.ppermute(leaving, 'section', swap)  6.84 us
    pallas_call x1, Pallas kernels, pack(): pl.pallas_call(pack_kernel, out_shape=jax.ShapeDtypeStruct(pool.shape, BF...  4.97 us
    ppermute x1, starting transfers between devices, body(): theirs = lax.ppermute(leaving, 'section', swap)  2.47 us
    ppermute x1, waiting for transfers between devices, body(): other = lax.ppermute(sent, 'section', swap)  2.3 us
    pallas_call x1, Pallas kernels, select(): pl.pallas_call(functools.partial(select_kernel, slots_dev=count, held=hel...  1.8 us
  transfers between devices with their start and end apart: 4, of which 3 were waited for; matrix products, arithmetic and copies ran while one was open for 2% of the time, Pallas kernels for 48%

profile of v4, /device:TPU:6, one launch (start us, length us, event | category | flops | bytes accessed | tf_op | source)
XLA Modules:
  0.0 64.7 jit_solution(9642173900550493659)
XLA Ops:
  0.6 1.5 %edge_rows.1.edge_hbm = bf16[16,2560]{1,0:T(8,128)(2,1)} custom-call(bf16[1024,2048]{1,0:T(8,128)(2,1)} %bitcast.23, bf16[1024,2,256]{2,1,0:T(2,128)(2,1)} %bitcast.32), custom_call_target="tpu_custom_call" | custom-call | bytes 262144 | tf_op jit(solution)/shard_map/edge_rows/pallas_call | solution.py:75
  2.2 0.0 copy-start.2
  2.2 1.4 %collective-permute-start = (bf16[16,2560]{1,0:T(8,128)(2,1)}, bf16[16,2560]{1,0:T(8,128)(2,1)S(1)}, u32[]{:S(2)}, u32[]{:S(2)}) collective-permute-start(bf16[16,2560]{1,0:T(8,128)(2,1)} %edge_rows.1.edge_hbm), channel_id=1, source_target_pairs={{0,64},{1,65},{2,66},{3,67},{4,68},{5,69},{6,70},{7,71},{8,72},{9,... | collective-permute-start | bytes 245768 | tf_op jit(solution)/shard_map/ppermute | solution.py:545
  3.6 5.0 %pack_states.1 = bf16[128,64,128]{2,1,0:T(8,128)(2,1)} custom-call(s32[16,128]{1,0:T(8,128)} %slots_ref.3, f32[128,64,128]{2,1,0:T(8,128)} %pool_hbm.1, bf16[16,2560]{1,0:T(8,128)(2,1)} %edge_rows.1.edge_hbm), custom_call_target="tpu_custom_call" | custom-call | bytes 6291456 | tf_op jit(solution)/shard_map/pack_states/pallas_call | solution.py:151
  8.6 0.3 collective-permute-done.got_x_ref.got_bc_ref
  8.8 0.0 copy-start.3
  8.8 11.5 %all-to-all-start = ((bf16[64,128,128]{2,1,0:T(8,128)(2,1)}), bf16[64,128,128]{2,1,0:T(8,128)(2,1)S(1)}, u32[]{:S(2)}, u32[]{:S(2)}) async-start(bf16[64,128,128]{2,1,0:T(8,128)(2,1)} %bitcast.30), calls=%async_computation | async-start | bytes 4194304 | tf_op jit(solution)/shard_map/all_to_all | solution.py:548
  21.0 0.0 copy-done.2
  21.0 1.3 %copy.22 = bf16[128,8,2,256]{3,1,2,0:T(8,128)(2,1)} copy(bf16[128,8,2,256]{3,2,1,0:T(2,128)(2,1)S(1)} %bitcast.33) | data formatting | bytes 2097152
  22.3 0.0 copy-done.3
  22.3 10.4 %local_blocks.2 = (bf16[1024,2048]{1,0:T(8,128)(2,1)}, bf16[1024,2048]{1,0:T(8,128)(2,1)}, bf16[1024,256]{1,0:T(8,128)(2,1)}, bf16[144,1024]{1,0:T(8,128)(2,1)S(1)}) custom-call(s32[1]{0:T(128)S(6)} %sub.3.group_ref, s32[1]{0:T(128)S(6)} %copy.27.len_ref, bf16[1024,2048]{1,0:T(8,128)(2,1)} %bitcast.24, bf16[1024,2048]{1,0:T(8,128)(2,1)} %bitcast.26, ...), custom_call_target="tpu_custom_call" | custom-call | flops 2147483648 | bytes 10485760 | tf_op jit(solution)/shard_map/local_blocks/pallas_call | solution.py:368
  32.7 2.5 %collective-permute-start.1 = (bf16[144,1024]{1,0:T(8,128)(2,1)S(1)}, bf16[144,1024]{1,0:T(8,128)(2,1)S(1)}, u32[]{:S(2)}, u32[]{:S(2)}) collective-permute-start(bf16[144,1024]{1,0:T(8,128)(2,1)S(1)} %get-tuple-element.28), channel_id=1, source_target_pairs={{0,64},{64,0},{1,65},{65,1},{2,66},{66,2},{3,67},{67,3},{4,68},{68... | collective-permute-start | bytes 884744 | tf_op jit(solution)/shard_map/ppermute | solution.py:561
  35.1 0.0 copy-start
  35.1 0.0 copy-start.1
  35.1 10.4 %local_blocks.3 = (bf16[1024,2048]{1,0:T(8,128)(2,1)}, bf16[1024,2048]{1,0:T(8,128)(2,1)}, bf16[1024,256]{1,0:T(8,128)(2,1)}, bf16[144,1024]{1,0:T(8,128)(2,1)S(1)}) custom-call(s32[1]{0:T(128)} %bitcast.group_ref, s32[1]{0:T(128)S(6)} %copy.27.len_ref, bf16[1024,2048]{1,0:T(8,128)(2,1)} %bitcast.25, ...), custom_call_target="tpu_custom_call", output_to_operand_aliasing={{0}: (16, {}), {1}: (17, {}), {2}: (18, {})} | custom-call | flops 2147483648 | bytes 10485760 | tf_op jit(solution)/shard_map/local_blocks/pallas_call | solution.py:368
  45.5 6.8 %collective-permute-done.1.theirs_ref.rest_2_ = bf16[144,1024]{1,0:T(8,128)(2,1)S(1)} collective-permute-done((bf16[144,1024]{1,0:T(8,128)(2,1)S(1)}, bf16[144,1024]{1,0:T(8,128)(2,1)S(1)}, u32[]{:S(2)}, u32[]{:S(2)}) %collective-permute-start.1) | collective-permute-done | bytes 294944 | tf_op jit(solution)/shard_map/ppermute | solution.py:561
  52.3 0.0 all-to-all-done
  52.3 0.0 copy-done
  52.4 1.8 %select_states.1 = (bf16[128,1024]{1,0:T(8,128)(2,1)S(1)}, bf16[128,1024]{1,0:T(8,128)(2,1)S(1)}) custom-call(s32[16,128]{1,0:T(8,128)S(1)} %copy-done, bf16[128,64,128]{2,1,0:T(8,128)(2,1)S(1)} %bitcast.20, bf16[144,1024]{1,0:T(8,128)(2,1)S(1)} %get-tuple-element.27.mine_ref.rest_1_, bf16[144,1024]{1,0:T(8,128)(2,1)S(1)} %collective-permute-done.1.theirs_ref.rest_2_), custom_call_target="tpu_custom_call" | custom-call | bytes 3145728 | tf_op jit(solution)/shard_map/select_states/pallas_call | solution.py:221
  54.2 0.1 collective-permute-start.2
  54.3 0.0 copy-done.1
  54.3 5.5 %join_blocks.2 = (bf16[1024,2048]{1,0:T(8,128)(2,1)}, f32[1024,128]{1,0:T(8,128)}, bf16[1024,1024]{1,0:T(8,128)(2,1)S(1)}, bf16[1024,1024]{1,0:T(8,128)(2,1)S(1)}, bf16[1024,128]{1,0:T(8,128)(2,1)S(1)}) custom-call(s32[1]{0:T(128)} %bitcast.group_ref, s32[1]{0:T(128)S(6)} %copy.27.len_ref, bf16[1024,2048]{1,0:T(8,128)(2,1)} %get-tuple-element.23.a_ref.rest_3_, ...), custom_call_target="tpu_custom_call" | custom-call | flops 268435456 | bytes 7340032 | tf_op jit(solution)/shard_map/join_blocks/pallas_call | solution.py:487
  59.8 2.3 %collective-permute-done.2.start = bf16[128,1024]{1,0:T(8,128)(2,1)S(1)} collective-permute-done((bf16[128,1024]{1,0:T(8,128)(2,1)S(1)}, bf16[128,1024]{1,0:T(8,128)(2,1)S(1)}, u32[]{:S(2)}, u32[]{:S(2)}) %collective-permute-start.2) | collective-permute-done | bytes 262176 | tf_op jit(solution)/shard_map/ppermute | solution.py:568
  62.1 2.6 %join_blocks.3 = bf16[1024,2048]{1,0:T(8,128)(2,1)} custom-call(s32[1]{0:T(128)S(6)} %sub.3.group_ref, s32[1]{0:T(128)S(6)} %copy.27.len_ref, bf16[1024,1024]{1,0:T(8,128)(2,1)S(1)} %get-tuple-element.31.a_ref, bf16[1024,1024]{1,0:T(8,128)(2,1)S(1)} %get-tuple-element.32.b_ref, ...), custom_call_target="tpu_custom_call", output_to_operand_aliasing={{}: (7, {})} | custom-call | flops 268435456 | bytes 7340032 | tf_op jit(solution)/shard_map/join_blocks/pallas_call | solution.py:487
Async XLA Ops:
  2.2 18.8 %copy-start.2 = (bf16[1,1024,2,256]{3,2,1,0:T(2,128)(2,1)S(1)}, bf16[1,1024,2,256]{3,2,1,0:T(2,128)(2,1)}, u32[]{:S(2)}) copy-start(bf16[1,1024,2,256]{3,2,1,0:T(2,128)(2,1)} %param.18) | copy-start | bytes 3145732
  2.2 6.7 %collective-permute-start = (bf16[16,2560]{1,0:T(8,128)(2,1)}, bf16[16,2560]{1,0:T(8,128)(2,1)S(1)}, u32[]{:S(2)}, u32[]{:S(2)}) collective-permute-start(bf16[16,2560]{1,0:T(8,128)(2,1)} %edge_rows.1.edge_hbm), channel_id=1, source_target_pairs={{0,64},{1,65},{2,66},{3,67},{4,68},{5,69},{6,70},{7,71},{8,72},{9,... | collective-permute-start | bytes 245768 | tf_op jit(solution)/shard_map/ppermute | solution.py:545
  8.8 13.4 %copy-start.3 = (bf16[16,2560]{1,0:T(8,128)(2,1)}, bf16[16,2560]{1,0:T(8,128)(2,1)S(1)}, u32[]{:S(2)}) copy-start(bf16[16,2560]{1,0:T(8,128)(2,1)S(1)} %collective-permute-done.got_x_ref.got_bc_ref) | copy-start | bytes 245764
  8.8 43.5 %all-to-all-start = ((bf16[64,128,128]{2,1,0:T(8,128)(2,1)}), bf16[64,128,128]{2,1,0:T(8,128)(2,1)S(1)}, u32[]{:S(2)}, u32[]{:S(2)}) async-start(bf16[64,128,128]{2,1,0:T(8,128)(2,1)} %bitcast.30), calls=%async_computation | async-start | bytes 4194304 | tf_op jit(solution)/shard_map/all_to_all | solution.py:548
  32.7 19.7 %collective-permute-start.1 = (bf16[144,1024]{1,0:T(8,128)(2,1)S(1)}, bf16[144,1024]{1,0:T(8,128)(2,1)S(1)}, u32[]{:S(2)}, u32[]{:S(2)}) collective-permute-start(bf16[144,1024]{1,0:T(8,128)(2,1)S(1)} %get-tuple-element.28), channel_id=1, source_target_pairs={{0,64},{64,0},{1,65},{65,1},{2,66},{66,2},{3,67},{67,3},{4,68},{68... | collective-permute-start | bytes 884744 | tf_op jit(solution)/shard_map/ppermute | solution.py:561
  35.1 17.2 %copy-start = (s32[16,128]{1,0:T(8,128)S(1)}, s32[16,128]{1,0:T(8,128)}, u32[]{:S(2)}) copy-start(s32[16,128]{1,0:T(8,128)} %slots_ref.3) | copy-start | bytes 24580
  35.1 19.1 %copy-start.1 = (f32[2048]{0:T(1024)S(1)}, f32[2048]{0:T(1024)}, u32[]{:S(2)}) copy-start(f32[2048]{0:T(1024)} %param.28) | copy-start | bytes 24580
  54.2 7.9 %collective-permute-start.2 = (bf16[128,1024]{1,0:T(8,128)(2,1)S(1)}, bf16[128,1024]{1,0:T(8,128)(2,1)S(1)}, u32[]{:S(2)}, u32[]{:S(2)}) collective-permute-start(bf16[128,1024]{1,0:T(8,128)(2,1)S(1)} %get-tuple-element.30.rest_0_), channel_id=1, source_target_pairs={{0,64},{64,0},{1,65},{65,1},{2,66},{66,2},{3,67},{67,3},{4,68},{68... | collective-permute-start | bytes 786440 | tf_op jit(solution)/shard_map/ppermute | solution.py:568
